TPU v7x, 32 devices: a whole 2x2x4 slice. The times are simulated.
32 devices in a mesh: row: 8 (over z, core), col: 4 (over y, x).
Axes of the slice: x: 2, y: 2, z: 4, core: 2. Of those that a mesh axis runs over, the one named last changes fastest.
Arguments:
- cells: float32 [1024, 1024], P(('row', 'col')), may hold values from 0 to 1
- instance_cell: int32 [32, 128], P('row', 'col'), may hold values from 0 to 1023, as said below
- target: float32 [1024, 4096], P('row', 'col'), may hold values from 0 to 1
- row_taps: float32 [8, 65], replicated, may hold values from -0.75 to 0.75
- col_taps: float32 [8, 65], replicated, may hold values from -0.75 to 0.75
- kernel_weight: float32 [8], replicated, may hold values from 0.05 to 0.5
Outputs:
- cells_out: float32 [1024, 1024], P(('row', 'col'))
Inputs may be any that keep to these rules, and one draw needn't show every extreme that they name: `instance_cell`: each entry is the index of the device that holds the cell, along row+col with row slowest, times 32, plus the cell's place there. Tile (a, b) lies on device (a // 4, b // 32). Among one device's tiles at most 8 name cells held by any one device, and one holding device is named by exactly 8 tiles of every device.
All inputs are finite; a program needn't handle non-finite values.
Results may differ from a plain program's by a relative error of at most 0.00016.
Values sent between devices are 32-bit elements; how exact they have to be, the bound alone decides.
No kernel may reach another device: no remote copies, remote signals or barrier semaphores. Data moves between devices by JAX's collectives and lax.ppermute only.
A program may use at most 128 MiB of HBM per device.

v0:
```python
import jax
import jax.numpy as jnp
from jax import lax
from jax.experimental import pallas as pl
from jax.experimental.pallas import tpu as pltpu
from jax.sharding import Mesh
from jax.sharding import PartitionSpec as P

TILE = 32
TAPS = 65
HALF = 32
KERNELS = 8
LANES = 128
WIDE = 256

STEEPNESS = 4.0
THRESHOLD = 0.3
STEP_RATE = 0.5

F32 = jnp.float32
BF16 = jnp.bfloat16


def split(x):
    high = x.astype(BF16)
    return high, (x - high.astype(F32)).astype(BF16)


def mm(a, b):
    return jnp.dot(a, b, preferred_element_type=F32)


def bands_kernel(wave_ref, fcol_ref, frow_ref, brow_ref, bcol_ref):
    rows = lax.broadcasted_iota(jnp.int32, (LANES, LANES), 0)
    lanes = lax.broadcasted_iota(jnp.int32, (LANES, LANES), 1)
    zero = jnp.zeros((LANES, LANES), F32)

    def circular(index, start):
        base = jnp.broadcast_to(wave_ref[pl.ds(index, 1), :], (LANES, LANES))
        return pltpu.roll(base, start, 1, stride=1, stride_axis=0)

    def put(ref, kernel, r0, c0, block, height=LANES, breadth=LANES):
        high, low = split(block)
        ref[kernel, 0, r0 : r0 + height, c0 : c0 + breadth] = high[:height, :breadth]
        ref[kernel, 1, r0 : r0 + height, c0 : c0 + breadth] = low[:height, :breadth]

    @pl.loop(0, KERNELS)
    def _(k):
        near = circular(k, 0)
        put(frow_ref, k, 0, 0, jnp.where(lanes >= rows, near, zero))
        put(frow_ref, k, 0, LANES, jnp.where(lanes < rows, near, zero))
        put(frow_ref, k, LANES, 0, zero, 64)
        put(frow_ref, k, LANES, LANES, jnp.where(lanes >= rows, near, zero), 64)
        near = circular(2 * KERNELS + k, 0)
        put(brow_ref, k, 0, 0, jnp.where(lanes >= rows, near, zero))
        put(brow_ref, k, 0, LANES, jnp.where(lanes < rows, near, zero))
        near = circular(3 * KERNELS + k, LANES // 2)
        put(fcol_ref, k, 0, 0, jnp.where(rows >= lanes, near, zero))
        put(fcol_ref, k, LANES, 0, jnp.where(rows < lanes, near, zero))
        near = circular(KERNELS + k, LANES // 2)
        low = jnp.where(rows >= lanes, near, zero)
        high = jnp.where(rows < lanes, near, zero)
        put(bcol_ref, k, 0, 0, low)
        put(bcol_ref, k, LANES, 0, high)
        put(bcol_ref, k, 2 * LANES, 0, zero)
        put(bcol_ref, k, 0, LANES, zero)
        put(bcol_ref, k, LANES, LANES, low)
        put(bcol_ref, k, 2 * LANES, LANES, high)


def make_bands(row_taps, col_taps):
    taps = jnp.concatenate([row_taps, col_taps], axis=0)
    taps = jnp.concatenate([taps, taps[:, ::-1]], axis=0)
    wave = jnp.pad(taps, [(0, 0), (0, LANES - TAPS)])
    shapes = [
        (KERNELS, 2, 256, LANES),
        (KERNELS, 2, 192, 256),
        (KERNELS, 2, LANES, 256),
        (KERNELS, 2, 384, 256),
    ]
    return pl.pallas_call(
        bands_kernel,
        out_shape=[jax.ShapeDtypeStruct(s, BF16) for s in shapes],
        in_specs=[pl.BlockSpec(memory_space=pltpu.VMEM)],
        out_specs=[pl.BlockSpec(memory_space=pltpu.VMEM)] * 4,
        compiler_params=pltpu.CompilerParams(vmem_limit_bytes=40 * 2**20),
        name="bands",
    )(wave)


def transpose_blocks(parts, block):
    turned = []
    for d in range(4):
        x = parts[d]
        for s in range(1, 4):
            x = jnp.where(block == s, parts[(s + d) % 4], x)
        turned.append(pltpu.roll(x, 32 * d, 1) if d else x)
    out = []
    for s in range(4):
        x = turned[(-s) % 4]
        for b in range(1, 4):
            x = jnp.where(block == b, turned[(b - s) % 4], x)
        out.append(x)
    return out


def pack_kernel(asked_ref, cells_ref, out_ref):
    def place(n):
        asked = jnp.maximum(asked_ref[n], 0)
        tile = cells_ref[pl.ds((asked // 8) * 64 + asked % 8, 8, stride=8), :]
        out_ref[pl.ds(pl.multiple_of(n * 8, 8), 8), :] = tile

    @pl.loop(0, asked_ref.shape[0] // 8)
    def _(group):
        for n in range(8):
            place(group * 8 + n)


def merge_kernel(asked_ref, tiles_ref, out_ref):
    out_ref[...] = jnp.zeros_like(out_ref)
    nothing = jnp.zeros((8, LANES), F32)

    def place(n):
        asked = asked_ref[n]
        tile = tiles_ref[pl.ds(pl.multiple_of(n * 8, 8), 8), :]
        cell = jnp.maximum(asked, 0)
        there = pl.ds((cell // 8) * 64 + cell % 8, 8, stride=8)
        out_ref[there, :] += jnp.where(asked >= 0, tile, nothing)

    @pl.loop(0, asked_ref.shape[0] // 8)
    def _(group):
        for n in range(8):
            place(group * 8 + n)


def step_kernel(cells_ref, sums_ref, out_ref):
    own = cells_ref.shape[0]
    total = sums_ref[:own, :]
    for d in range(1, sums_ref.shape[0] // own):
        total = total + sums_ref[d * own : (d + 1) * own, :]
    out_ref[...] = cells_ref[...] - STEP_RATE * total


def assemble_kernel(index_ref, tiles_ref, target_ref, mask_ref, first_ref, last_ref, turned_ref):
    tile_rows, tile_cols = index_ref.shape
    height = tile_rows * TILE
    groups = tile_cols // 4
    block = lax.broadcasted_iota(jnp.int32, (8, LANES), 1) // 32

    @pl.loop(0, tile_rows)
    def _(a):
        for g in range(groups):
            parts = [
                tiles_ref[pl.ds(pl.multiple_of(index_ref[a, 4 * g + b] * 8, 8), 8), :]
                for b in range(4)
            ]
            for s, piece in enumerate(transpose_blocks(parts, block)):
                turned_ref[pl.ds(g * height + a * TILE + s, 8, stride=4), :] = piece

    for g in range(groups):
        lanes = slice(LANES * g, LANES * (g + 1))
        piece = turned_ref[g * height : (g + 1) * height, :]
        mask_ref[:, lanes] = piece
        first_ref[: 2 * HALF, lanes] = piece[: 2 * HALF]
        last_ref[: 2 * HALF, lanes] = piece[height - 2 * HALF :]
    first_ref[2 * HALF :, :] = target_ref[:HALF, :]
    last_ref[2 * HALF :, :] = target_ref[height - HALF :, :]


def edges_kernel(mask_ref, target_ref, top_ref, bottom_ref, first_ref, last_ref):
    height, breadth = mask_ref.shape
    wide = 2 * HALF
    for ref, lanes in ((first_ref, slice(0, LANES)), (last_ref, slice(breadth - LANES, breadth))):
        ref[:wide, :] = top_ref[:wide, lanes]
        ref[wide : wide + height, :] = mask_ref[:, lanes]
        ref[wide + height : 2 * wide + height, :] = bottom_ref[:wide, lanes]
        start = 2 * wide + height
        ref[start : start + HALF, :] = top_ref[wide:, lanes]
        ref[start + HALF : start + HALF + height, :] = target_ref[:, lanes]
        ref[start + HALF + height :, :] = bottom_ref[wide:, lanes]


def image_kernel(
    index_ref,
    where_ref,
    weight_ref,
    mask_ref,
    own_ref,
    top_ref,
    bottom_ref,
    before_ref,
    after_ref,
    fcol_ref,
    frow_ref,
    brow_ref,
    bcol_ref,
    out_ref,
    mhigh_ref,
    mlow_ref,
    target_ref,
    field_ref,
    ghigh_ref,
    glow_ref,
    grad_ref,
):
    tile_rows, tile_cols = index_ref.shape
    rows_here = tile_rows * TILE
    high_rows = rows_here + 4 * HALF
    field_rows = rows_here + 2 * HALF
    groups = tile_cols // 4
    wide = 2 * HALF
    block = lax.broadcasted_iota(jnp.int32, (8, LANES), 1) // 32

    def shifted(shift, parts, edge, emit):
        for rows, ref, start, count in parts:
            lane = lax.broadcasted_iota(jnp.int32, (count, LANES), 1)
            turned = None
            for g in range(groups + 2):
                if g == 0:
                    piece = before_ref[edge + rows : edge + rows + count, :]
                elif g == groups + 1:
                    piece = after_ref[edge + rows : edge + rows + count, :]
                else:
                    piece = ref[start : start + count, LANES * (g - 1) : LANES * g]
                fresh = pltpu.roll(piece, shift, 1)
                if g:
                    emit(rows, count, g - 1, jnp.where(lane < shift, turned, fresh))
                turned = fresh

    def put_mask(rows, count, g, piece):
        high, low = split(piece)
        mhigh_ref[rows : rows + count, LANES * g : LANES * (g + 1)] = high
        mlow_ref[rows : rows + count, LANES * g : LANES * (g + 1)] = low

    def put_target(rows, count, g, piece):
        target_ref[rows : rows + count, LANES * g : LANES * (g + 1)] = piece

    shifted(
        wide,
        (
            (0, top_ref, 0, wide),
            (wide, mask_ref, 0, rows_here),
            (wide + rows_here, bottom_ref, 0, wide),
        ),
        0,
        put_mask,
    )
    shifted(
        HALF,
        (
            (0, top_ref, wide, HALF),
            (HALF, own_ref, 0, rows_here),
            (HALF + rows_here, bottom_ref, wide, HALF),
        ),
        high_rows,
        put_target,
    )
    for g in range(groups + 1, mhigh_ref.shape[1] // LANES):
        lanes = slice(LANES * g, LANES * (g + 1))
        mhigh_ref[:, lanes] = jnp.zeros((high_rows, LANES), BF16)
        mlow_ref[:, lanes] = jnp.zeros((high_rows, LANES), BF16)

    def columns(offset, width):
        def window(ref, j):
            return ref[:, pl.ds(pl.multiple_of(offset + j * LANES, LANES), WIDE)]

        blocks = width // LANES
        stacked = jnp.concatenate(
            [
                jnp.concatenate(
                    [window(mhigh_ref, j), window(mlow_ref, j), window(mhigh_ref, j)], axis=1
                )
                for j in range(blocks)
            ],
            axis=0,
        )
        intensity = None
        for pair in range(KERNELS // 2):
            two = [
                jnp.concatenate([fcol_ref[2 * pair, v], fcol_ref[2 * pair + 1, v]], axis=1)
                for v in range(2)
            ]
            wide = mm(stacked, jnp.concatenate([two[0], two[0], two[1]], axis=0))
            for h in range(2):
                k = 2 * pair + h
                half = jnp.concatenate(
                    [
                        wide[j * high_rows : (j + 1) * high_rows, h * LANES : (h + 1) * LANES]
                        for j in range(blocks)
                    ],
                    axis=1,
                )
                high, low = split(half)
                field = mm(
                    jnp.concatenate([frow_ref[k, 0], frow_ref[k, 0], frow_ref[k, 1]], axis=1),
                    jnp.concatenate([high, low, high], axis=0),
                )
                field_ref[k, :, :width] = field
                term = weight_ref[k] * field * field
                intensity = term if intensity is None else intensity + term
        resist = 1.0 / (1.0 + jnp.exp(-STEEPNESS * (intensity - THRESHOLD)))
        target = target_ref[:, pl.ds(pl.multiple_of(offset, LANES), width)]
        sensitivity = 2.0 * (resist - target) * STEEPNESS * resist * (1.0 - resist)
        row = where_ref[0] + lax.broadcasted_iota(jnp.int32, (field_rows, width), 0)
        col = where_ref[1] + offset + lax.broadcasted_iota(jnp.int32, (field_rows, width), 1)
        inside = (row >= 0) & (row < where_ref[2]) & (col >= 0) & (col < where_ref[3])
        sensitivity = jnp.where(inside, sensitivity, 0.0)
        for k in range(KERNELS):
            product = (2.0 * weight_ref[k]) * sensitivity * field_ref[k, :, :width]
            high, low = split(product)
            near = brow_ref[k, 0, :, :192]
            part = mm(near, high) + (mm(near, low) + mm(brow_ref[k, 1, :, :192], high))
            high, low = split(part)
            place = pl.ds(pl.multiple_of(offset, LANES), width)
            ghigh_ref[k, :, place] = high
            glow_ref[k, :, place] = low

    supers = tile_cols * TILE // WIDE

    @pl.loop(0, supers)
    def _(jj):
        columns(jj * WIDE, WIDE)

    columns(supers * WIDE, LANES)

    def spread_back(k):
        def window(ref, jj):
            return ref[k, :, WIDE * jj : WIDE * jj + 384]

        stacked = jnp.concatenate(
            [
                jnp.concatenate(
                    [window(ghigh_ref, jj), window(glow_ref, jj), window(ghigh_ref, jj)], axis=1
                )
                for jj in range(supers)
            ],
            axis=0,
        )
        return mm(
            stacked, jnp.concatenate([bcol_ref[k, 0], bcol_ref[k, 0], bcol_ref[k, 1]], axis=0)
        )

    def add(part, fresh):
        for g in range(groups):
            rows = slice(g * rows_here, (g + 1) * rows_here)
            top = (g // 2) * rows_here
            piece = part[top : top + rows_here, LANES * (g % 2) : LANES * (g % 2 + 1)]
            grad_ref[rows, :] = piece if fresh else grad_ref[rows, :] + piece

    add(spread_back(0), True)

    @pl.loop(1, KERNELS)
    def _(k):
        add(spread_back(k), False)

    @pl.loop(0, tile_rows)
    def _(a):
        for g in range(groups):
            base = g * rows_here + a * TILE
            parts = [grad_ref[pl.ds(base + s, 8, stride=4), :] for s in range(4)]
            for b, tile in enumerate(transpose_blocks(parts, block)):
                place = pl.multiple_of(index_ref[a, 4 * g + b] * 8, 8)
                out_ref[pl.ds(place, 8), :] = tile


def to_rows(x):
    count = x.shape[0]
    return x.reshape(count // 8, 8, 8, LANES).transpose(0, 2, 1, 3).reshape(count * 8, LANES)


def from_rows(x):
    count = x.shape[0] // 8
    return x.reshape(count // 8, 8, 8, LANES).transpose(0, 2, 1, 3).reshape(count, 8 * LANES)


def kernel_call(body, name, shapes, scratch, scalars, inputs, megabytes=40):
    single = not isinstance(shapes, list)
    spec = pl.BlockSpec(memory_space=pltpu.VMEM)
    outs = [shapes] if single else shapes
    result = pl.pallas_call(
        body,
        out_shape=outs,
        in_specs=[pl.BlockSpec(memory_space=pltpu.SMEM)] * len(scalars) + [spec] * len(inputs),
        out_specs=[spec] * len(outs),
        scratch_shapes=scratch,
        compiler_params=pltpu.CompilerParams(vmem_limit_bytes=megabytes * 2**20),
        name=name,
    )(*scalars, *inputs)
    return result[0] if single else result


def neighbours(first, last, axis):
    count = lax.axis_size(axis)
    up = [(i, i + 1) for i in range(count - 1)]
    down = [(j, i) for i, j in up]
    return lax.ppermute(last, axis, up), lax.ppermute(first, axis, down)


def shards(cells, instance_cell, target, row_taps, col_taps, kernel_weight):
    deep, cores, cols = lax.axis_size("deep"), lax.axis_size("core"), lax.axis_size("col")
    plane = ("core", "col")
    peers = cores * cols
    slots = cells.shape[0]
    tile_rows, tile_cols = instance_cell.shape
    tiles_here = tile_rows * tile_cols
    height, breadth = target.shape
    owners = deep * peers
    capacity = min(tiles_here, deep * 2 * ((tiles_here + owners - 1) // owners))
    f32 = lambda *shape: jax.ShapeDtypeStruct(shape, F32)

    named = instance_cell.reshape(-1)
    owner = named // slots
    peer = owner % peers
    local = (owner // peers) * slots + named % slots
    same = (peer[:, None] == peer[None, :]) & jnp.tri(tiles_here, k=-1, dtype=bool)
    position = peer * capacity + jnp.sum(same.astype(jnp.int32), axis=1)
    request = jnp.max(
        jnp.where(position[None, :] == jnp.arange(peers * capacity)[:, None], local[None, :], -1),
        axis=1,
    )
    asked = lax.all_to_all(request, plane, split_axis=0, concat_axis=0, tiled=True)

    flat = to_rows(cells)
    copies = jnp.broadcast_to(flat[None], (deep,) + flat.shape).reshape(-1, LANES)
    stack = lax.all_to_all(copies, "deep", split_axis=0, concat_axis=0, tiled=True)
    packed = kernel_call(
        pack_kernel, "pack", f32(peers * capacity * 8, LANES), [], [asked], [stack]
    )
    arrived = lax.all_to_all(packed, plane, split_axis=0, concat_axis=0, tiled=True)
    index = position.reshape(tile_rows, tile_cols)
    mask, first, last = kernel_call(
        assemble_kernel,
        "assemble",
        [f32(height, breadth), f32(3 * HALF, breadth), f32(3 * HALF, breadth)],
        [pltpu.VMEM((height * (breadth // LANES), LANES), F32)],
        [index],
        [arrived, target],
    )
    top, bottom = neighbours(first, last, ("deep", "core"))
    edge_rows = 2 * height + 6 * HALF
    first, last = kernel_call(
        edges_kernel,
        "edges",
        [f32(edge_rows, LANES), f32(edge_rows, LANES)],
        [],
        [],
        [mask, target, top, bottom],
    )
    before, after = neighbours(first, last, "col")
    my_row = lax.axis_index(("deep", "core"))
    my_col = lax.axis_index("col")
    where = jnp.stack(
        [
            my_row * height - HALF,
            my_col * breadth - HALF,
            jnp.int32(deep * cores * height),
            jnp.int32(cols * breadth),
        ]
    ).astype(jnp.int32)
    bands = make_bands(row_taps, col_taps)
    field_rows = height + 2 * HALF
    returned = kernel_call(
        image_kernel,
        "image",
        f32(peers * capacity * 8, LANES),
        [
            pltpu.VMEM((height + 4 * HALF, breadth + 256), BF16),
            pltpu.VMEM((height + 4 * HALF, breadth + 256), BF16),
            pltpu.VMEM((field_rows, breadth + 128), F32),
            pltpu.VMEM((KERNELS, field_rows, WIDE), F32),
            pltpu.VMEM((KERNELS, height, breadth + 128), BF16),
            pltpu.VMEM((KERNELS, height, breadth + 128), BF16),
            pltpu.VMEM((height * (breadth // LANES), LANES), F32),
        ],
        [index, where, kernel_weight],
        [mask, target, top, bottom, before, after, *bands],
        56,
    )
    back = lax.all_to_all(returned, plane, split_axis=0, concat_axis=0, tiled=True)
    merged = kernel_call(merge_kernel, "merge", f32(deep * slots * 8, LANES), [], [asked], [back])
    parts = lax.all_to_all(merged, "deep", split_axis=0, concat_axis=0, tiled=True)
    return from_rows(kernel_call(step_kernel, "step", f32(slots * 8, LANES), [], [], [flat, parts]))


def solution(mesh):
    rows, cols = mesh.devices.shape
    finer = Mesh(mesh.devices.reshape(rows // 2, 2, cols), ("deep", "core", "col"))
    row = ("deep", "core")
    placed = (P((*row, "col"), None), P(row, "col"), P(row, "col"), P(), P(), P())
    return jax.shard_map(
        shards, mesh=finer, in_specs=placed, out_specs=P((*row, "col"), None), check_vma=False
    )
```

profile of v0, /device:TPU:0, one launch (start us, length us, event | category | flops | bytes accessed | tf_op | source)
XLA Modules:
  0.0 147.8 jit_solution(14750713985439564618)
XLA Ops:
  0.0 0.8 reshape.169
  0.9 0.2 convert_reduce_fusion
  1.1 0.1 select_reduce_fusion
  1.3 9.6 %all_to_all.52 = s32[8,32,1]{1,2,0:T(1,128)S(1)} all-to-all(s32[8,32,1]{1,2,0:T(1,128)S(1)} %bitcast.29), channel_id=1, replica_groups=mesh['deep'=4,'core'=2,'col'=4] {'core','col'}, dimensions={0} | all-to-all | bytes 2048 | tf_op jit(solution)/shard_map/all_to_all | solution.py:421
  10.9 1.7 %broadcast_in_dim.24 = f32[4,256,128]{2,1,0:T(8,128)} broadcast(f32[256,128]{1,0:T(8,128)} %bitcast.26), dimensions={1,2} | broadcast | bytes 655360 | tf_op jit(solution)/shard_map/broadcast_in_dim | solution.py:424
  12.6 4.9 %all-to-all-start.1 = ((f32[4,256,128]{2,1,0:T(8,128)}), f32[4,256,128]{2,1,0:T(8,128)S(1)}, u32[]{:S(2)}, u32[]{:S(2)}) async-start(f32[4,256,128]{2,1,0:T(8,128)} %broadcast_in_dim.24), calls=%async_computation.1 | async-start | bytes 1048576 | tf_op jit(solution)/shard_map/all_to_all | solution.py:425
  17.5 0.5 broadcast.271
  18.0 0.7 reduce.3
  18.7 13.2 %all-to-all-done.1 = f32[4,256,128]{2,1,0:T(8,128)S(1)} async-done(((f32[4,256,128]{2,1,0:T(8,128)}), f32[4,256,128]{2,1,0:T(8,128)S(1)}, u32[]{:S(2)}, u32[]{:S(2)}) %all-to-all-start.1) | async-done | bytes 524320 | tf_op jit(solution)/shard_map/all_to_all | solution.py:425
  32.0 2.7 %pack.1 = f32[2048,128]{1,0:T(8,128)} custom-call(s32[256]{0:T(256)S(1)} %all_to_all.35.asked_ref, f32[1024,128]{1,0:T(8,128)S(1)} %bitcast.24), custom_call_target="tpu_custom_call" | custom-call | tf_op jit(solution)/shard_map/pack/pallas_call | solution.py:380
  34.7 3.7 %all-to-all-start.2 = ((f32[8,256,128]{2,1,0:T(8,128)}), f32[8,256,128]{2,1,0:T(8,128)S(1)}, u32[]{:S(2)}, u32[]{:S(2)}) async-start(f32[8,256,128]{2,1,0:T(8,128)} %bitcast.9), calls=%async_computation.2 | async-start | bytes 2097152 | tf_op jit(solution)/shard_map/all_to_all | solution.py:429
  38.5 14.7 %all-to-all-done.2 = f32[8,256,128]{2,1,0:T(8,128)S(1)} async-done(((f32[8,256,128]{2,1,0:T(8,128)}), f32[8,256,128]{2,1,0:T(8,128)S(1)}, u32[]{:S(2)}, u32[]{:S(2)}) %all-to-all-start.2) | async-done | bytes 1048608 | tf_op jit(solution)/shard_map/all_to_all | solution.py:429
  53.2 1.1 assemble.1
  54.4 2.2 %collective-permute-start = (f32[96,1024]{1,0:T(8,128)S(1)}, f32[96,1024]{1,0:T(8,128)S(1)}, u32[]{:S(2)}, u32[]{:S(2)}) collective-permute-start(f32[96,1024]{1,0:T(8,128)S(1)} %get-tuple-element.15), channel_id=1, source_target_pairs={{0,4},{4,8},{8,12},{12,16},{16,20},{20,24},{24,28},{1,5},{5,9},{9,... | collective-permute-start | bytes 1179656 | tf_op jit(solution)/shard_map/ppermute | solution.py:396
  56.6 1.3 collective-permute-start.1
  57.9 2.3 %collective-permute-done.1.bottom_ref = f32[96,1024]{1,0:T(8,128)S(1)} collective-permute-done((f32[96,1024]{1,0:T(8,128)S(1)}, f32[96,1024]{1,0:T(8,128)S(1)}, u32[]{:S(2)}, u32[]{:S(2)}) %collective-permute-start.1) | collective-permute-done | bytes 393248 | tf_op jit(solution)/shard_map/ppermute | solution.py:396
  60.2 2.7 %collective-permute-start.2 = (f32[448,128]{1,0:T(8,128)S(1)}, f32[448,128]{1,0:T(8,128)S(1)}, u32[]{:S(2)}, u32[]{:S(2)}) collective-permute-start(f32[448,128]{1,0:T(8,128)S(1)} %get-tuple-element.17), channel_id=1, source_target_pairs={{0,1},{1,2},{2,3},{4,5},{5,6},{6,7},{8,9},{9,10},{10,11},{12,13},{... | collective-permute-start | bytes 688136 | tf_op jit(solution)/shard_map/ppermute | solution.py:396
  63.0 1.3 collective-permute-start.3
  64.4 1.6 %bands.1 = (bf16[8,2,256,128]{3,2,1,0:T(8,128)(2,1)S(1)}, bf16[8,2,192,256]{3,2,1,0:T(8,128)(2,1)S(1)}, bf16[8,2,128,256]{3,2,1,0:T(8,128)(2,1)S(1)}, bf16[8,2,384,256]{3,2,1,0:T(8,128)(2,1)S(1)}) custom-call(f32[32,128]{1,0:T(8,128)S(1)} %select_maximum_fusion.wave_ref), custom_call_target="tpu_custom_call" | custom-call | tf_op jit(solution)/shard_map/bands/pallas_call | solution.py:81
  66.1 1.6 %copy-done.1 = bf16[8,2,384,256]{3,2,1,0:T(8,128)(2,1)} copy-done((bf16[8,2,384,256]{3,2,1,0:T(8,128)(2,1)}, bf16[8,2,384,256]{3,2,1,0:T(8,128)(2,1)S(1)}, u32[]{:S(2)}) %copy-start.1) | copy-done | bytes 3145752
  67.7 1.2 copy-done.5
  68.9 1.0 copy-done.6
  69.9 1.0 copy-done.7
  70.8 0.6 pad_add_fusion.where_ref
  71.4 0.3 collective-permute-done.3.after_ref
  71.7 0.4 copy-done.10
  72.1 0.3 copy-done.11
  72.4 29.0 %image.1 = f32[2048,128]{1,0:T(8,128)} custom-call(s32[4,32]{1,0:T(4,128)} %copy-done.9, s32[4]{0:T(128)} %pad_add_fusion.where_ref, f32[8]{0:T(128)} %weight_ref.1, f32[128,1024]{1,0:T(8,128)} %copy-done.2, f32[128,1024]{1,0:T(8,128)} %own_ref.1, f32[96,1024]{1,0:T(8,128)} %copy-done.3, f32[96,1024]{1,0:T(8,128)} %copy-done.4, f32[448,128]{1,0:T(8,128)} %copy-done.10, ...), custom_call_target="tpu_custom_call" | custom-call | tf_op jit(solution)/shard_map/image/pallas_call | solution.py:380
  101.4 23.8 %all_to_all.53 = f32[8,256,128]{2,1,0:T(8,128)S(1)} all-to-all(f32[8,256,128]{2,1,0:T(8,128)} %bitcast.28), channel_id=1, replica_groups=mesh['deep'=4,'core'=2,'col'=4] {'core','col'}, dimensions={0} | all-to-all | bytes 2097152 | tf_op jit(solution)/shard_map/all_to_all | solution.py:479
  125.2 2.4 %merge.1 = f32[1024,128]{1,0:T(8,128)S(1)} custom-call(s32[256]{0:T(256)S(1)} %all_to_all.35.asked_ref, f32[2048,128]{1,0:T(8,128)S(1)} %bitcast.22), custom_call_target="tpu_custom_call" | custom-call | tf_op jit(solution)/shard_map/merge/pallas_call | solution.py:380
  127.6 19.5 %all_to_all.54 = f32[4,256,128]{2,1,0:T(8,128)S(1)} all-to-all(f32[4,256,128]{2,1,0:T(8,128)S(1)} %bitcast.25), channel_id=1, replica_groups=mesh['deep'=4,'core'=2,'col'=4] {'deep'}, dimensions={0} | all-to-all | bytes 1048576 | tf_op jit(solution)/shard_map/all_to_all | solution.py:481
  147.1 0.7 step.1
  (37 shorter events, 0.5 us)
Async XLA Ops:
  0.0 38.5 %copy-start.14 = (s32[4,32]{1,0:T(4,128)S(1)}, s32[4,32]{1,0:T(4,128)}, u32[]{:S(2)}) copy-start(s32[4,32]{1,0:T(4,128)} %param.7) | copy-start | bytes 1540
  0.0 53.2 %copy-start = (f32[128,1024]{1,0:T(8,128)S(1)}, f32[128,1024]{1,0:T(8,128)}, u32[]{:S(2)}) copy-start(f32[128,1024]{1,0:T(8,128)} %own_ref.1) | copy-start | bytes 1572868
  12.6 19.4 %all-to-all-start.1 = ((f32[4,256,128]{2,1,0:T(8,128)}), f32[4,256,128]{2,1,0:T(8,128)S(1)}, u32[]{:S(2)}, u32[]{:S(2)}) async-start(f32[4,256,128]{2,1,0:T(8,128)} %broadcast_in_dim.24), calls=%async_computation.1 | async-start | bytes 1048576 | tf_op jit(solution)/shard_map/all_to_all | solution.py:425
  34.7 29.6 %copy-start.12 = (f32[8,65]{1,0:T(8,128)S(1)}, f32[8,65]{1,0:T(8,128)}, u32[]{:S(2)}) copy-start(f32[8,65]{1,0:T(8,128)} %param.10) | copy-start | bytes 6244
  34.7 29.6 %copy-start.13 = (f32[8,65]{1,0:T(8,128)S(1)}, f32[8,65]{1,0:T(8,128)}, u32[]{:S(2)}) copy-start(f32[8,65]{1,0:T(8,128)} %param.9) | copy-start | bytes 6244
  34.7 18.5 %all-to-all-start.2 = ((f32[8,256,128]{2,1,0:T(8,128)}), f32[8,256,128]{2,1,0:T(8,128)S(1)}, u32[]{:S(2)}, u32[]{:S(2)}) async-start(f32[8,256,128]{2,1,0:T(8,128)} %bitcast.9), calls=%async_computation.2 | async-start | bytes 2097152 | tf_op jit(solution)/shard_map/all_to_all | solution.py:429
  38.5 33.2 %copy-start.9 = (s32[4,32]{1,0:T(4,128)}, s32[4,32]{1,0:T(4,128)S(1)}, u32[]{:S(2)}) copy-start(s32[4,32]{1,0:T(4,128)S(1)} %fusion.4.index_ref) | copy-start | bytes 1540
  54.4 17.4 %copy-start.2 = (f32[128,1024]{1,0:T(8,128)}, f32[128,1024]{1,0:T(8,128)S(1)}, u32[]{:S(2)}) copy-start(f32[128,1024]{1,0:T(8,128)S(1)} %get-tuple-element.14.mask_ref) | copy-start | bytes 1572868
  54.4 3.5 %collective-permute-start = (f32[96,1024]{1,0:T(8,128)S(1)}, f32[96,1024]{1,0:T(8,128)S(1)}, u32[]{:S(2)}, u32[]{:S(2)}) collective-permute-start(f32[96,1024]{1,0:T(8,128)S(1)} %get-tuple-element.15), channel_id=1, source_target_pairs={{0,4},{4,8},{8,12},{12,16},{16,20},{20,24},{24,28},{1,5},{5,9},{9,... | collective-permute-start | bytes 1179656 | tf_op jit(solution)/shard_map/ppermute | solution.py:396
  56.6 3.6 %collective-permute-start.1 = (f32[96,1024]{1,0:T(8,128)S(1)}, f32[96,1024]{1,0:T(8,128)S(1)}, u32[]{:S(2)}, u32[]{:S(2)}) collective-permute-start(f32[96,1024]{1,0:T(8,128)S(1)} %get-tuple-element.16), channel_id=1, source_target_pairs={{4,0},{8,4},{12,8},{16,12},{20,16},{24,20},{28,24},{5,1},{9,5},{13... | collective-permute-start | bytes 1179656 | tf_op jit(solution)/shard_map/ppermute | solution.py:396
  57.9 13.8 %copy-start.3 = (f32[96,1024]{1,0:T(8,128)}, f32[96,1024]{1,0:T(8,128)S(1)}, u32[]{:S(2)}) copy-start(f32[96,1024]{1,0:T(8,128)S(1)} %collective-permute-done.top_ref) | copy-start | bytes 1179652
  60.2 11.5 %copy-start.4 = (f32[96,1024]{1,0:T(8,128)}, f32[96,1024]{1,0:T(8,128)S(1)}, u32[]{:S(2)}) copy-start(f32[96,1024]{1,0:T(8,128)S(1)} %collective-permute-done.1.bottom_ref) | copy-start | bytes 1179652
  60.2 11.2 %collective-permute-start.2 = (f32[448,128]{1,0:T(8,128)S(1)}, f32[448,128]{1,0:T(8,128)S(1)}, u32[]{:S(2)}, u32[]{:S(2)}) collective-permute-start(f32[448,128]{1,0:T(8,128)S(1)} %get-tuple-element.17), channel_id=1, source_target_pairs={{0,1},{1,2},{2,3},{4,5},{5,6},{6,7},{8,9},{9,10},{10,11},{12,13},{... | collective-permute-start | bytes 688136 | tf_op jit(solution)/shard_map/ppermute | solution.py:396
  63.0 8.7 %collective-permute-start.3 = (f32[448,128]{1,0:T(8,128)S(1)}, f32[448,128]{1,0:T(8,128)S(1)}, u32[]{:S(2)}, u32[]{:S(2)}) collective-permute-start(f32[448,128]{1,0:T(8,128)S(1)} %get-tuple-element.18), channel_id=1, source_target_pairs={{1,0},{2,1},{3,2},{5,4},{6,5},{7,6},{9,8},{10,9},{11,10},{13,12},{... | collective-permute-start | bytes 688136 | tf_op jit(solution)/shard_map/ppermute | solution.py:396
  66.0 1.6 %copy-start.1 = (bf16[8,2,384,256]{3,2,1,0:T(8,128)(2,1)}, bf16[8,2,384,256]{3,2,1,0:T(8,128)(2,1)S(1)}, u32[]{:S(2)}) copy-start(bf16[8,2,384,256]{3,2,1,0:T(8,128)(2,1)S(1)} %get-tuple-element.22.bcol_ref) | copy-start | bytes 9437188
  67.7 1.2 copy-start.5
  68.8 1.0 copy-start.6
  69.9 1.0 copy-start.7
  71.4 0.7 copy-start.10
  71.7 0.7 copy-start.11
  101.4 45.7 %copy-start.8 = (f32[32,1024]{1,0:T(8,128)S(1)}, f32[32,1024]{1,0:T(8,128)}, u32[]{:S(2)}) copy-start(f32[32,1024]{1,0:T(8,128)} %param.6) | copy-start | bytes 393220
where the time goes:
time: 148 us
  blocking collectives  52.9 us (36%)
  Pallas kernels  37.6 us (25%)
  waiting for transfers between devices  30.5 us (21%)
  starting transfers between devices  16.1 us (11%)
  local copies, waits for them, and re-layouts  8.89 us (6%)
  other arithmetic  1.58 us (1%)
    pallas_call x6, Pallas kernels, kernel_call(): pl.pallas_call(body, out_shape=outs, in_specs=[pl.BlockSpec(memory_space=...  36 us
    all_to_all x1, blocking collectives, shards(): lax.all_to_all(returned, plane, split_axis=0, concat_axis=0, tiled=True)  23.8 us
    all_to_all x1, blocking collectives, shards(): lax.all_to_all(merged, 'deep', split_axis=0, concat_axis=0, tiled=True)  19.5 us
    all_to_all x1, waiting for transfers between devices, shards(): lax.all_to_all(packed, plane, split_axis=0, concat_axis=0, tiled=True)  14.7 us
    all_to_all x1, waiting for transfers between devices, shards(): lax.all_to_all(copies, 'deep', split_axis=0, concat_axis=0, tiled=True)  13.2 us
    all_to_all x1, blocking collectives, shards(): lax.all_to_all(request, plane, split_axis=0, concat_axis=0, tiled=True)  9.62 us
    ppermute x4, starting transfers between devices, neighbours(): return (lax.ppermute(last, axis, up), lax.ppermute(first, axis, down))  7.53 us
    unnamed x30, local copies, waits for them, and re-layouts  5.51 us
  transfers between devices with their start and end apart: 6, of which 4 were waited for; matrix products, arithmetic and copies ran while one was open for 1% of the time, Pallas kernels for 1%

commit v1 on v0

--- a/solution.py
+++ b/solution.py
@@ -83,7 +83,7 @@
         out_shape=[jax.ShapeDtypeStruct(s, BF16) for s in shapes],
         in_specs=[pl.BlockSpec(memory_space=pltpu.VMEM)],
         out_specs=[pl.BlockSpec(memory_space=pltpu.VMEM)] * 4,
-        compiler_params=pltpu.CompilerParams(vmem_limit_bytes=40 * 2**20),
+        compiler_params=pltpu.CompilerParams(vmem_limit_bytes=16 * 2**20),
         name="bands",
     )(wave)
 
@@ -104,41 +104,49 @@
     return out
 
 
-def pack_kernel(asked_ref, cells_ref, out_ref):
-    def place(n):
-        asked = jnp.maximum(asked_ref[n], 0)
-        tile = cells_ref[pl.ds((asked // 8) * 64 + asked % 8, 8, stride=8), :]
-        out_ref[pl.ds(pl.multiple_of(n * 8, 8), 8), :] = tile
-
-    @pl.loop(0, asked_ref.shape[0] // 8)
-    def _(group):
-        for n in range(8):
-            place(group * 8 + n)
-
-
-def merge_kernel(asked_ref, tiles_ref, out_ref):
-    out_ref[...] = jnp.zeros_like(out_ref)
+def spread_kernel(cells_ref, out_ref):
+    own = cells_ref.shape[0]
+    for c in range(own // 8):
+        tile = cells_ref[pl.ds((c // 8) * 64 + c % 8, 8, stride=8), :]
+        for d in range(out_ref.shape[0] // own):
+            out_ref[d * own + c * 8 : d * own + c * 8 + 8, :] = tile
+
+
+def pack_kernel(asked_ref, me_ref, cells_ref, early_ref, out_ref):
+    peers, capacity = asked_ref.shape
+
+    @pl.loop(0, peers)
+    def _(i):
+        base = (me_ref[0] ^ i) * capacity
+        for j in range(capacity):
+            asked = jnp.maximum(asked_ref[i, j], 0)
+            tile = cells_ref[pl.ds(pl.multiple_of(asked * 8, 8), 8), :]
+            out_ref[pl.ds(pl.multiple_of((base + j) * 8, 8), 8), :] = tile
+
+
+def step_kernel(asked_ref, me_ref, cells_ref, tiles_ref, out_ref, *totals):
+    owners, capacity = asked_ref.shape
     nothing = jnp.zeros((8, LANES), F32)
-
-    def place(n):
-        asked = asked_ref[n]
-        tile = tiles_ref[pl.ds(pl.multiple_of(n * 8, 8), 8), :]
-        cell = jnp.maximum(asked, 0)
-        there = pl.ds((cell // 8) * 64 + cell % 8, 8, stride=8)
-        out_ref[there, :] += jnp.where(asked >= 0, tile, nothing)
-
-    @pl.loop(0, asked_ref.shape[0] // 8)
-    def _(group):
-        for n in range(8):
-            place(group * 8 + n)
-
-
-def step_kernel(cells_ref, sums_ref, out_ref):
-    own = cells_ref.shape[0]
-    total = sums_ref[:own, :]
-    for d in range(1, sums_ref.shape[0] // own):
-        total = total + sums_ref[d * own : (d + 1) * own, :]
-    out_ref[...] = cells_ref[...] - STEP_RATE * total
+    for total in totals:
+        total[...] = jnp.zeros_like(total)
+
+    @pl.loop(0, owners)
+    def _(i):
+        base = (me_ref[1] ^ i) * capacity
+        for j in range(capacity):
+            asked = asked_ref[i, j]
+            tile = tiles_ref[pl.ds(pl.multiple_of((base + j) * 8, 8), 8), :]
+            there = pl.ds(pl.multiple_of(jnp.maximum(asked, 0) * 8, 8), 8)
+            total = totals[j % len(totals)]
+            total[there, :] += jnp.where(asked >= 0, tile, nothing)
+
+    for c in range(out_ref.shape[0] // 8):
+        rows = slice(c * 8, c * 8 + 8)
+        total = totals[0][rows, :]
+        for other in totals[1:]:
+            total = total + other[rows, :]
+        there = pl.ds((c // 8) * 64 + c % 8, 8, stride=8)
+        out_ref[there, :] = cells_ref[there, :] - STEP_RATE * total
 
 
 def assemble_kernel(index_ref, tiles_ref, target_ref, mask_ref, first_ref, last_ref, turned_ref):
@@ -291,10 +299,8 @@
                     axis=1,
                 )
                 high, low = split(half)
-                field = mm(
-                    jnp.concatenate([frow_ref[k, 0], frow_ref[k, 0], frow_ref[k, 1]], axis=1),
-                    jnp.concatenate([high, low, high], axis=0),
-                )
+                both = mm(jnp.concatenate([frow_ref[k, 0], frow_ref[k, 1]], axis=0), high)
+                field = both[:field_rows] + both[field_rows:] + mm(frow_ref[k, 0], low)
                 field_ref[k, :, :width] = field
                 term = weight_ref[k] * field * field
                 intensity = term if intensity is None else intensity + term
@@ -308,8 +314,9 @@
         for k in range(KERNELS):
             product = (2.0 * weight_ref[k]) * sensitivity * field_ref[k, :, :width]
             high, low = split(product)
-            near = brow_ref[k, 0, :, :192]
-            part = mm(near, high) + (mm(near, low) + mm(brow_ref[k, 1, :, :192], high))
+            near = brow_ref[k, 0, :, :field_rows]
+            both = mm(jnp.concatenate([near, brow_ref[k, 1, :, :field_rows]], axis=0), high)
+            part = both[:rows_here] + both[rows_here:] + mm(near, low)
             high, low = split(part)
             place = pl.ds(pl.multiple_of(offset, LANES), width)
             ghigh_ref[k, :, place] = high
@@ -373,19 +380,21 @@
     return x.reshape(count // 8, 8, 8, LANES).transpose(0, 2, 1, 3).reshape(count, 8 * LANES)
 
 
-def kernel_call(body, name, shapes, scratch, scalars, inputs, megabytes=40):
+def kernel_call(body, name, shapes, scratch, scalars, inputs, megabytes, unread=()):
     single = not isinstance(shapes, list)
     spec = pl.BlockSpec(memory_space=pltpu.VMEM)
     outs = [shapes] if single else shapes
     result = pl.pallas_call(
         body,
         out_shape=outs,
-        in_specs=[pl.BlockSpec(memory_space=pltpu.SMEM)] * len(scalars) + [spec] * len(inputs),
+        in_specs=[pl.BlockSpec(memory_space=pltpu.SMEM)] * len(scalars)
+        + [spec] * len(inputs)
+        + [pl.BlockSpec(memory_space=pl.ANY)] * len(unread),
         out_specs=[spec] * len(outs),
         scratch_shapes=scratch,
         compiler_params=pltpu.CompilerParams(vmem_limit_bytes=megabytes * 2**20),
         name=name,
-    )(*scalars, *inputs)
+    )(*scalars, *inputs, *unread)
     return result[0] if single else result
 
 
@@ -396,8 +405,25 @@
     return lax.ppermute(last, axis, up), lax.ppermute(first, axis, down)
 
 
+def doubled(table, axis):
+    count = lax.axis_size(axis)
+    bit = 1
+    while bit < count:
+        got = lax.ppermute(table, axis, [(i, i ^ bit) for i in range(count)])
+        table = jnp.concatenate([table, got], axis=0)
+        bit *= 2
+    return table
+
+
+def requests(match, value, capacity):
+    rank = jnp.cumsum(match.astype(jnp.int32), axis=1) - 1
+    hit = match[:, None, :] & (rank[:, None, :] == jnp.arange(capacity)[None, :, None])
+    return jnp.max(jnp.where(hit, value[:, None, :], -1), axis=2)
+
+
 def shards(cells, instance_cell, target, row_taps, col_taps, kernel_weight):
     deep, cores, cols = lax.axis_size("deep"), lax.axis_size("core"), lax.axis_size("col")
+    everyone = ("deep", "core", "col")
     plane = ("core", "col")
     peers = cores * cols
     slots = cells.shape[0]
@@ -405,36 +431,54 @@
     tiles_here = tile_rows * tile_cols
     height, breadth = target.shape
     owners = deep * peers
-    capacity = min(tiles_here, deep * 2 * ((tiles_here + owners - 1) // owners))
+    capacity = 2 * ((tiles_here + owners - 1) // owners)
+    wide_capacity = min(tiles_here, deep * capacity)
     f32 = lambda *shape: jax.ShapeDtypeStruct(shape, F32)
 
-    named = instance_cell.reshape(-1)
-    owner = named // slots
-    peer = owner % peers
-    local = (owner // peers) * slots + named % slots
-    same = (peer[:, None] == peer[None, :]) & jnp.tri(tiles_here, k=-1, dtype=bool)
-    position = peer * capacity + jnp.sum(same.astype(jnp.int32), axis=1)
-    request = jnp.max(
-        jnp.where(position[None, :] == jnp.arange(peers * capacity)[:, None], local[None, :], -1),
-        axis=1,
-    )
-    asked = lax.all_to_all(request, plane, split_axis=0, concat_axis=0, tiled=True)
-
     flat = to_rows(cells)
-    copies = jnp.broadcast_to(flat[None], (deep,) + flat.shape).reshape(-1, LANES)
+    copies = kernel_call(
+        spread_kernel, "spread", f32(deep * slots * 8, LANES), [], [], [flat], 8
+    )
     stack = lax.all_to_all(copies, "deep", split_axis=0, concat_axis=0, tiled=True)
+
+    named = instance_cell.reshape(1, -1)
+    near = doubled(doubled(named, "col"), "core")
+    me = jnp.stack([lax.axis_index(plane), lax.axis_index(everyone)]).astype(jnp.int32)
+    owner = near // slots
+    asked = requests(
+        owner % peers == me[0], (owner // peers) * slots + near % slots, wide_capacity
+    )
+    bands = make_bands(row_taps, col_taps)
     packed = kernel_call(
-        pack_kernel, "pack", f32(peers * capacity * 8, LANES), [], [asked], [stack]
+        pack_kernel,
+        "pack",
+        f32(peers * wide_capacity * 8, LANES),
+        [],
+        [asked, me],
+        [stack],
+        8,
+        [bands[0]],
     )
     arrived = lax.all_to_all(packed, plane, split_axis=0, concat_axis=0, tiled=True)
-    index = position.reshape(tile_rows, tile_cols)
+
+    everything = doubled(near, "deep")
+    wanted = requests(everything // slots == me[1], everything % slots, capacity)
+    mine = named[0] // slots
+    earlier = jnp.tri(tiles_here, k=-1, dtype=bool)
+
+    def place(group, size):
+        same = (group[:, None] == group[None, :]) & earlier
+        where = group * size + jnp.sum(same.astype(jnp.int32), axis=1)
+        return where.reshape(tile_rows, tile_cols)
+
     mask, first, last = kernel_call(
         assemble_kernel,
         "assemble",
         [f32(height, breadth), f32(3 * HALF, breadth), f32(3 * HALF, breadth)],
         [pltpu.VMEM((height * (breadth // LANES), LANES), F32)],
-        [index],
+        [place(mine % peers, wide_capacity)],
         [arrived, target],
+        8,
     )
     top, bottom = neighbours(first, last, ("deep", "core"))
     edge_rows = 2 * height + 6 * HALF
@@ -445,6 +489,7 @@
         [],
         [],
         [mask, target, top, bottom],
+        8,
     )
     before, after = neighbours(first, last, "col")
     my_row = lax.axis_index(("deep", "core"))
@@ -457,12 +502,11 @@
             jnp.int32(cols * breadth),
         ]
     ).astype(jnp.int32)
-    bands = make_bands(row_taps, col_taps)
     field_rows = height + 2 * HALF
     returned = kernel_call(
         image_kernel,
         "image",
-        f32(peers * capacity * 8, LANES),
+        f32(owners * capacity * 8, LANES),
         [
             pltpu.VMEM((height + 4 * HALF, breadth + 256), BF16),
             pltpu.VMEM((height + 4 * HALF, breadth + 256), BF16),
@@ -472,14 +516,21 @@
             pltpu.VMEM((KERNELS, height, breadth + 128), BF16),
             pltpu.VMEM((height * (breadth // LANES), LANES), F32),
         ],
-        [index, where, kernel_weight],
+        [place(mine, capacity), where, kernel_weight],
         [mask, target, top, bottom, before, after, *bands],
-        56,
-    )
-    back = lax.all_to_all(returned, plane, split_axis=0, concat_axis=0, tiled=True)
-    merged = kernel_call(merge_kernel, "merge", f32(deep * slots * 8, LANES), [], [asked], [back])
-    parts = lax.all_to_all(merged, "deep", split_axis=0, concat_axis=0, tiled=True)
-    return from_rows(kernel_call(step_kernel, "step", f32(slots * 8, LANES), [], [], [flat, parts]))
+        32,
+    )
+    back = lax.all_to_all(returned, everyone, split_axis=0, concat_axis=0, tiled=True)
+    stepped = kernel_call(
+        step_kernel,
+        "step",
+        f32(slots * 8, LANES),
+        [pltpu.VMEM((slots * 8, LANES), F32)] * 4,
+        [wanted, me],
+        [flat, back],
+        8,
+    )
+    return from_rows(stepped)
 
 
 def solution(mesh):

time: 148 us -> 136 us (0.919)
  blocking collectives: 52.9 us -> 0 us
  starting transfers between devices: 16.1 us -> 36.6 us
  waiting for transfers between devices: 30.5 us -> 49.2 us
  local copies, waits for them, and re-layouts: 8.89 us -> 13 us
  Pallas kernels: 37.6 us -> 33.5 us
  other arithmetic: 1.58 us -> 3.31 us
    all_to_all x3 -> x0, blocking collectives: 52.9 us -> none  [the longest x1 23.8 us: shards(): lax.all_to_all(returned, plane, split_axis=0, concat_axis=0, tiled=True)]
    ppermute x0 -> x5, waiting for transfers between devices: none -> 21.4 us  [doubled(): got = lax.ppermute(table, axis, [(i, i ^ bit) for i in range(count)])]
    ppermute x0 -> x5, starting transfers between devices: none -> 11.1 us  [doubled(): got = lax.ppermute(table, axis, [(i, i ^ bit) for i in range(count)])]
    all_to_all x1, waiting for transfers between devices: 13.2 us -> 3.6 us  [shards(): lax.all_to_all(copies, 'deep', split_axis=0, concat_axis=0, tiled=True)]
    all_to_all x0 -> x1, starting transfers between devices: none -> 9.24 us  [shards(): lax.all_to_all(returned, everyone, split_axis=0, concat_axis=0, tiled=True)]
    ppermute x4, waiting for transfers between devices: 2.6 us -> 9.85 us  [neighbours(): return (lax.ppermute(last, axis, up), lax.ppermute(first, axis, down))]
    unnamed x30 -> x28, local copies, waits for them, and re-layouts: 5.51 us -> 11.8 us
    pallas_call x6, Pallas kernels: 36 us -> 31.9 us  [kernel_call(): pl.pallas_call(body, out_shape=outs, in_specs=[pl.BlockSpec(memory_space=...]
  transfers between devices with their start and end apart: 6 -> 12, of which waited for: 4 -> 8; matrix products, arithmetic and copies ran while one was open for 1% -> 3% of each run, Pallas kernels for 1% -> 2%
where the time goes in v1:
time: 136 us
  waiting for transfers between devices  49.2 us (36%)
  starting transfers between devices  36.6 us (27%)
  Pallas kernels  33.5 us (25%)
  local copies, waits for them, and re-layouts  13 us (10%)
  other arithmetic  3.31 us (2%)
    pallas_call x6, Pallas kernels, kernel_call(): pl.pallas_call(body, out_shape=outs, in_specs=[pl.BlockSpec(memory_space=...  31.9 us
    ppermute x5, waiting for transfers between devices, doubled(): got = lax.ppermute(table, axis, [(i, i ^ bit) for i in range(count)])  21.4 us
    all_to_all x1, waiting for transfers between devices, shards(): lax.all_to_all(packed, plane, split_axis=0, concat_axis=0, tiled=True)  14.3 us
    unnamed x28, local copies, waits for them, and re-layouts  11.8 us
    ppermute x5, starting transfers between devices, doubled(): got = lax.ppermute(table, axis, [(i, i ^ bit) for i in range(count)])  11.1 us
    ppermute x4, waiting for transfers between devices, neighbours(): return (lax.ppermute(last, axis, up), lax.ppermute(first, axis, down))  9.85 us
    all_to_all x1, starting transfers between devices, shards(): lax.all_to_all(returned, everyone, split_axis=0, concat_axis=0, tiled=True)  9.24 us
    ppermute x4, starting transfers between devices, neighbours(): return (lax.ppermute(last, axis, up), lax.ppermute(first, axis, down))  7.51 us
  transfers between devices with their start and end apart: 12, of which 8 were waited for; matrix products, arithmetic and copies ran while one was open for 3% of the time, Pallas kernels for 2%

profile of v1, /device:TPU:0, one launch (start us, length us, event | category | flops | bytes accessed | tf_op | source)
XLA Modules:
  0.0 135.7 jit_solution(6567709860377463601)
XLA Ops:
  0.8 2.9 %collective-permute-start = (s32[1,128]{1,0:T(1,128)S(1)}, s32[1,128]{1,0:T(1,128)S(1)}, u32[]{:S(2)}, u32[]{:S(2)}) collective-permute-start(s32[1,128]{1,0:T(1,128)S(1)} %concatenate.108), channel_id=1, source_target_pairs={{0,1},{1,0},{2,3},{3,2},{4,5},{5,4},{6,7},{7,6},{8,9},{9,8},{10,11... | collective-permute-start | bytes 1544 | tf_op jit(solution)/shard_map/ppermute | solution.py:412
  5.5 5.0 %all-to-all-start = ((f32[4,256,128]{2,1,0:T(8,128)}), f32[4,256,128]{2,1,0:T(8,128)S(1)}, u32[]{:S(2)}, u32[]{:S(2)}) async-start(f32[4,256,128]{2,1,0:T(8,128)} %bitcast.9), calls=%async_computation | async-start | bytes 1048576 | tf_op jit(solution)/shard_map/all_to_all | solution.py:442
  11.3 1.6 %collective-permute-start.1 = (s32[2,128]{1,0:T(2,128)S(1)}, s32[2,128]{1,0:T(2,128)S(1)}, u32[]{:S(2)}, u32[]{:S(2)}) collective-permute-start(s32[2,128]{1,0:T(2,128)S(1)} %pad_add_fusion.2), channel_id=1, source_target_pairs={{0,2},{1,3},{2,0},{3,1},{4,6},{5,7},{6,4},{7,5},{8,10},{9,11},{10,... | collective-permute-start | bytes 3080 | tf_op jit(solution)/shard_map/ppermute | solution.py:412
  13.6 1.3 collective-permute-done.1
  15.1 1.6 %bands.1 = (bf16[8,2,256,128]{3,2,1,0:T(8,128)(2,1)S(1)}, bf16[8,2,192,256]{3,2,1,0:T(8,128)(2,1)S(1)}, bf16[8,2,128,256]{3,2,1,0:T(8,128)(2,1)S(1)}, bf16[8,2,384,256]{3,2,1,0:T(8,128)(2,1)S(1)}) custom-call(f32[32,128]{1,0:T(8,128)S(1)} %select_maximum_fusion.wave_ref), custom_call_target="tpu_custom_call" | custom-call | tf_op jit(solution)/shard_map/bands/pallas_call | solution.py:81
  16.7 1.6 %copy-done.2 = bf16[8,2,384,256]{3,2,1,0:T(8,128)(2,1)} copy-done((bf16[8,2,384,256]{3,2,1,0:T(8,128)(2,1)}, bf16[8,2,384,256]{3,2,1,0:T(8,128)(2,1)S(1)}, u32[]{:S(2)}) %copy-start.2) | copy-done | bytes 3145752
  18.3 1.2 copy-done.4
  19.5 1.0 copy-done.6
  21.1 3.6 %all-to-all-done = f32[4,256,128]{2,1,0:T(8,128)S(1)} async-done(((f32[4,256,128]{2,1,0:T(8,128)}), f32[4,256,128]{2,1,0:T(8,128)S(1)}, u32[]{:S(2)}, u32[]{:S(2)}) %all-to-all-start) | async-done | bytes 524320 | tf_op jit(solution)/shard_map/all_to_all | solution.py:442
  24.7 1.0 pack.1
  25.7 1.0 copy-done.1
  26.7 3.7 %all-to-all-start.1 = ((f32[8,256,128]{2,1,0:T(8,128)}), f32[8,256,128]{2,1,0:T(8,128)S(1)}, u32[]{:S(2)}, u32[]{:S(2)}) async-start(f32[8,256,128]{2,1,0:T(8,128)} %bitcast.22), calls=%async_computation.1 | async-start | bytes 2097152 | tf_op jit(solution)/shard_map/all_to_all | solution.py:462
  30.9 14.3 %all-to-all-done.1 = f32[8,256,128]{2,1,0:T(8,128)S(1)} async-done(((f32[8,256,128]{2,1,0:T(8,128)}), f32[8,256,128]{2,1,0:T(8,128)S(1)}, u32[]{:S(2)}, u32[]{:S(2)}) %all-to-all-start.1) | async-done | bytes 1048608 | tf_op jit(solution)/shard_map/all_to_all | solution.py:462
  45.2 1.1 assemble.1
  46.4 2.2 %collective-permute-start.5 = (f32[96,1024]{1,0:T(8,128)S(1)}, f32[96,1024]{1,0:T(8,128)S(1)}, u32[]{:S(2)}, u32[]{:S(2)}) collective-permute-start(f32[96,1024]{1,0:T(8,128)S(1)} %get-tuple-element.16), channel_id=1, source_target_pairs={{0,4},{4,8},{8,12},{12,16},{16,20},{20,24},{24,28},{1,5},{5,9},{9,... | collective-permute-start | bytes 1179656 | tf_op jit(solution)/shard_map/ppermute | solution.py:405
  48.6 1.3 collective-permute-start.6
  49.9 2.3 %collective-permute-done.6.bottom_ref = f32[96,1024]{1,0:T(8,128)S(1)} collective-permute-done((f32[96,1024]{1,0:T(8,128)S(1)}, f32[96,1024]{1,0:T(8,128)S(1)}, u32[]{:S(2)}, u32[]{:S(2)}) %collective-permute-start.6) | collective-permute-done | bytes 393248 | tf_op jit(solution)/shard_map/ppermute | solution.py:405
  53.0 2.7 %collective-permute-start.7 = (f32[448,128]{1,0:T(8,128)}, f32[448,128]{1,0:T(8,128)S(1)}, u32[]{:S(2)}, u32[]{:S(2)}) collective-permute-start(f32[448,128]{1,0:T(8,128)} %get-tuple-element.18), channel_id=1, source_target_pairs={{0,1},{1,2},{2,3},{4,5},{5,6},{6,7},{8,9},{9,10},{10,11},{12,13},{... | collective-permute-start | bytes 688136 | tf_op jit(solution)/shard_map/ppermute | solution.py:405
  55.7 1.3 collective-permute-start.8
  57.1 2.4 %collective-permute-done.7.before_ref = f32[448,128]{1,0:T(8,128)S(1)} collective-permute-done((f32[448,128]{1,0:T(8,128)}, f32[448,128]{1,0:T(8,128)S(1)}, u32[]{:S(2)}, u32[]{:S(2)}) %collective-permute-start.7) | collective-permute-done | bytes 229408 | tf_op jit(solution)/shard_map/ppermute | solution.py:405
  59.6 5.1 %collective-permute-done.8.after_ref = f32[448,128]{1,0:T(8,128)S(1)} collective-permute-done((f32[448,128]{1,0:T(8,128)}, f32[448,128]{1,0:T(8,128)S(1)}, u32[]{:S(2)}, u32[]{:S(2)}) %collective-permute-start.8) | collective-permute-done | bytes 229408 | tf_op jit(solution)/shard_map/ppermute | solution.py:405
  65.4 1.9 %copy-done.3 = bf16[8,2,384,256]{3,2,1,0:T(8,128)(2,1)S(1)} copy-done((bf16[8,2,384,256]{3,2,1,0:T(8,128)(2,1)S(1)}, bf16[8,2,384,256]{3,2,1,0:T(8,128)(2,1)}, u32[]{:S(2)}) %copy-start.3) | copy-done | bytes 3145752
  67.3 1.4 %copy-done.5 = bf16[8,2,192,256]{3,2,1,0:T(8,128)(2,1)S(1)} copy-done((bf16[8,2,192,256]{3,2,1,0:T(8,128)(2,1)S(1)}, bf16[8,2,192,256]{3,2,1,0:T(8,128)(2,1)}, u32[]{:S(2)}) %copy-start.5) | copy-done | bytes 1572888
  68.7 1.2 copy-done.7
  69.9 0.9 copy-done.11
  70.8 25.7 %image.1 = f32[2048,128]{1,0:T(8,128)} custom-call(s32[4,32]{1,0:T(4,128)S(1)} %get-tuple-element.34.index_ref, s32[4]{0:T(128)S(1)} %pad_add_fusion.4.where_ref, f32[8]{0:T(128)S(1)} %copy-done.12, f32[128,1024]{1,0:T(8,128)S(1)} %get-tuple-element.15.mask_ref, f32[128,1024]{1,0:T(8,128)S(1)} %copy-done, f32[96,1024]{1,0:T(8,128)S(1)} %collective-permute-done.5.top_ref, ...), custom_call_target="tpu_custom_call" | custom-call | tf_op jit(solution)/shard_map/image/pallas_call | solution.py:387
  96.5 9.2 %all-to-all-start.2 = ((f32[32,64,128]{2,1,0:T(8,128)}), f32[32,64,128]{2,1,0:T(8,128)S(1)}, u32[]{:S(2)}, u32[]{:S(2)}) async-start(f32[32,64,128]{2,1,0:T(8,128)} %bitcast.13), calls=%async_computation.2 | async-start | bytes 2097152 | tf_op jit(solution)/shard_map/all_to_all | solution.py:523
  105.7 2.0 %collective-permute-start.3 = (s32[8,128]{1,0:T(8,128)S(1)}, s32[8,128]{1,0:T(8,128)S(1)}, u32[]{:S(2)}, u32[]{:S(2)}) collective-permute-start(s32[8,128]{1,0:T(8,128)S(1)} %get-tuple-element.32), channel_id=1, source_target_pairs={{0,8},{8,0},{16,24},{24,16},{1,9},{9,1},{17,25},{25,17},{2,10},{10... | collective-permute-start | bytes 12296 | tf_op jit(solution)/shard_map/ppermute | solution.py:412
  107.8 15.8 %collective-permute-done.3 = s32[8,128]{1,0:T(8,128)S(1)} collective-permute-done((s32[8,128]{1,0:T(8,128)S(1)}, s32[8,128]{1,0:T(8,128)S(1)}, u32[]{:S(2)}, u32[]{:S(2)}) %collective-permute-start.3) | collective-permute-done | bytes 4128 | tf_op jit(solution)/shard_map/ppermute | solution.py:412
  123.6 4.5 %collective-permute-start.4 = (s32[16,128]{1,0:T(8,128)S(1)}, s32[16,128]{1,0:T(8,128)S(1)}, u32[]{:S(2)}, u32[]{:S(2)}) collective-permute-start(s32[16,128]{1,0:T(8,128)S(1)} %concatenate.112), channel_id=1, source_target_pairs={{0,16},{8,24},{16,0},{24,8},{1,17},{9,25},{17,1},{25,9},{2,18},{10... | collective-permute-start | bytes 24584 | tf_op jit(solution)/shard_map/ppermute | solution.py:412
  128.0 4.3 %collective-permute-done.4 = s32[16,128]{1,0:T(8,128)S(1)} collective-permute-done((s32[16,128]{1,0:T(8,128)S(1)}, s32[16,128]{1,0:T(8,128)S(1)}, u32[]{:S(2)}, u32[]{:S(2)}) %collective-permute-start.4) | collective-permute-done | bytes 8224 | tf_op jit(solution)/shard_map/ppermute | solution.py:412
  133.4 2.4 %step.1 = f32[256,128]{1,0:T(8,128)} custom-call(s32[32,8]{1,0:T(8,128)S(1)} %select_reduce_fusion.1.asked_ref, s32[2]{0:T(128)S(1)} %pad_add_fusion.3.me_ref, f32[256,128]{1,0:T(8,128)S(1)} %bitcast.25, f32[2048,128]{1,0:T(8,128)S(1)} %bitcast.20), custom_call_target="tpu_custom_call" | custom-call | tf_op jit(solution)/shard_map/step/pallas_call | solution.py:387
  (53 shorter events, 7.8 us)
Async XLA Ops:
  0.8 10.5 %collective-permute-start = (s32[1,128]{1,0:T(1,128)S(1)}, s32[1,128]{1,0:T(1,128)S(1)}, u32[]{:S(2)}, u32[]{:S(2)}) collective-permute-start(s32[1,128]{1,0:T(1,128)S(1)} %concatenate.108), channel_id=1, source_target_pairs={{0,1},{1,0},{2,3},{3,2},{4,5},{5,4},{6,7},{7,6},{8,9},{9,8},{10,11... | collective-permute-start | bytes 1544 | tf_op jit(solution)/shard_map/ppermute | solution.py:412
  3.7 0.9 copy-start.8
  4.6 25.8 %copy-start.13 = (s32[4,32]{1,0:T(4,128)S(1)}, s32[4,32]{1,0:T(4,128)}, u32[]{:S(2)}) copy-start(s32[4,32]{1,0:T(4,128)} %param.7) | copy-start | bytes 1540
  5.5 39.8 %copy-start = (f32[128,1024]{1,0:T(8,128)S(1)}, f32[128,1024]{1,0:T(8,128)}, u32[]{:S(2)}) copy-start(f32[128,1024]{1,0:T(8,128)} %own_ref.1) | copy-start | bytes 1572868
  5.5 19.2 %all-to-all-start = ((f32[4,256,128]{2,1,0:T(8,128)}), f32[4,256,128]{2,1,0:T(8,128)S(1)}, u32[]{:S(2)}, u32[]{:S(2)}) async-start(f32[4,256,128]{2,1,0:T(8,128)} %bitcast.9), calls=%async_computation | async-start | bytes 1048576 | tf_op jit(solution)/shard_map/all_to_all | solution.py:442
  11.3 3.6 %collective-permute-start.1 = (s32[2,128]{1,0:T(2,128)S(1)}, s32[2,128]{1,0:T(2,128)S(1)}, u32[]{:S(2)}, u32[]{:S(2)}) collective-permute-start(s32[2,128]{1,0:T(2,128)S(1)} %pad_add_fusion.2), channel_id=1, source_target_pairs={{0,2},{1,3},{2,0},{3,1},{4,6},{5,7},{6,4},{7,5},{8,10},{9,11},{10,... | collective-permute-start | bytes 3080 | tf_op jit(solution)/shard_map/ppermute | solution.py:412
  14.9 5.6 %collective-permute-start.2 = (s32[4,128]{1,0:T(4,128)S(1)}, s32[4,128]{1,0:T(4,128)S(1)}, u32[]{:S(2)}, u32[]{:S(2)}) collective-permute-start(s32[4,128]{1,0:T(4,128)S(1)} %pad_add_fusion.1), channel_id=1, source_target_pairs={{0,4},{4,0},{1,5},{5,1},{2,6},{6,2},{3,7},{7,3},{8,12},{12,8},{9,1... | collective-permute-start | bytes 6152 | tf_op jit(solution)/shard_map/ppermute | solution.py:412
  16.7 1.7 %copy-start.2 = (bf16[8,2,384,256]{3,2,1,0:T(8,128)(2,1)}, bf16[8,2,384,256]{3,2,1,0:T(8,128)(2,1)S(1)}, u32[]{:S(2)}) copy-start(bf16[8,2,384,256]{3,2,1,0:T(8,128)(2,1)S(1)} %get-tuple-element.22.bcol_ref) | copy-start | bytes 9437188
  18.3 1.2 copy-start.4
  19.5 1.0 copy-start.6
  25.7 1.0 copy-start.1
  26.7 38.6 %copy-start.12 = (f32[8]{0:T(128)S(1)}, f32[8]{0:T(128)}, u32[]{:S(2)}) copy-start(f32[8]{0:T(128)} %weight_ref.1) | copy-start | bytes 100
  26.7 18.5 %all-to-all-start.1 = ((f32[8,256,128]{2,1,0:T(8,128)}), f32[8,256,128]{2,1,0:T(8,128)S(1)}, u32[]{:S(2)}, u32[]{:S(2)}) async-start(f32[8,256,128]{2,1,0:T(8,128)} %bitcast.22), calls=%async_computation.1 | async-start | bytes 2097152 | tf_op jit(solution)/shard_map/all_to_all | solution.py:462
  46.4 3.5 %collective-permute-start.5 = (f32[96,1024]{1,0:T(8,128)S(1)}, f32[96,1024]{1,0:T(8,128)S(1)}, u32[]{:S(2)}, u32[]{:S(2)}) collective-permute-start(f32[96,1024]{1,0:T(8,128)S(1)} %get-tuple-element.16), channel_id=1, source_target_pairs={{0,4},{4,8},{8,12},{12,16},{16,20},{20,24},{24,28},{1,5},{5,9},{9,... | collective-permute-start | bytes 1179656 | tf_op jit(solution)/shard_map/ppermute | solution.py:405
  48.6 3.6 %collective-permute-start.6 = (f32[96,1024]{1,0:T(8,128)S(1)}, f32[96,1024]{1,0:T(8,128)S(1)}, u32[]{:S(2)}, u32[]{:S(2)}) collective-permute-start(f32[96,1024]{1,0:T(8,128)S(1)} %get-tuple-element.17), channel_id=1, source_target_pairs={{4,0},{8,4},{12,8},{16,12},{20,16},{24,20},{28,24},{5,1},{9,5},{13... | collective-permute-start | bytes 1179656 | tf_op jit(solution)/shard_map/ppermute | solution.py:405
  53.0 6.5 %collective-permute-start.7 = (f32[448,128]{1,0:T(8,128)}, f32[448,128]{1,0:T(8,128)S(1)}, u32[]{:S(2)}, u32[]{:S(2)}) collective-permute-start(f32[448,128]{1,0:T(8,128)} %get-tuple-element.18), channel_id=1, source_target_pairs={{0,1},{1,2},{2,3},{4,5},{5,6},{6,7},{8,9},{9,10},{10,11},{12,13},{... | collective-permute-start | bytes 688136 | tf_op jit(solution)/shard_map/ppermute | solution.py:405
  55.7 8.9 %collective-permute-start.8 = (f32[448,128]{1,0:T(8,128)}, f32[448,128]{1,0:T(8,128)S(1)}, u32[]{:S(2)}, u32[]{:S(2)}) collective-permute-start(f32[448,128]{1,0:T(8,128)} %get-tuple-element.19), channel_id=1, source_target_pairs={{1,0},{2,1},{3,2},{5,4},{6,5},{7,6},{9,8},{10,9},{11,10},{13,12},{... | collective-permute-start | bytes 688136 | tf_op jit(solution)/shard_map/ppermute | solution.py:405
  64.7 0.7 copy-start.10
  65.4 1.9 %copy-start.3 = (bf16[8,2,384,256]{3,2,1,0:T(8,128)(2,1)S(1)}, bf16[8,2,384,256]{3,2,1,0:T(8,128)(2,1)}, u32[]{:S(2)}) copy-start(bf16[8,2,384,256]{3,2,1,0:T(8,128)(2,1)} %copy-done.2) | copy-start | bytes 9437188
  67.3 1.4 %copy-start.5 = (bf16[8,2,192,256]{3,2,1,0:T(8,128)(2,1)S(1)}, bf16[8,2,192,256]{3,2,1,0:T(8,128)(2,1)}, u32[]{:S(2)}) copy-start(bf16[8,2,192,256]{3,2,1,0:T(8,128)(2,1)} %copy-done.4) | copy-start | bytes 4718596
  68.7 1.2 copy-start.7
  69.9 0.9 copy-start.11
  70.8 62.5 %copy-start.9 = (f32[32,1024]{1,0:T(8,128)S(1)}, f32[32,1024]{1,0:T(8,128)}, u32[]{:S(2)}) copy-start(f32[32,1024]{1,0:T(8,128)} %param.6) | copy-start | bytes 393220
  96.5 36.9 %all-to-all-start.2 = ((f32[32,64,128]{2,1,0:T(8,128)}), f32[32,64,128]{2,1,0:T(8,128)S(1)}, u32[]{:S(2)}, u32[]{:S(2)}) async-start(f32[32,64,128]{2,1,0:T(8,128)} %bitcast.13), calls=%async_computation.2 | async-start | bytes 2097152 | tf_op jit(solution)/shard_map/all_to_all | solution.py:523
  105.7 17.8 %collective-permute-start.3 = (s32[8,128]{1,0:T(8,128)S(1)}, s32[8,128]{1,0:T(8,128)S(1)}, u32[]{:S(2)}, u32[]{:S(2)}) collective-permute-start(s32[8,128]{1,0:T(8,128)S(1)} %get-tuple-element.32), channel_id=1, source_target_pairs={{0,8},{8,0},{16,24},{24,16},{1,9},{9,1},{17,25},{25,17},{2,10},{10... | collective-permute-start | bytes 12296 | tf_op jit(solution)/shard_map/ppermute | solution.py:412
  123.6 8.8 %collective-permute-start.4 = (s32[16,128]{1,0:T(8,128)S(1)}, s32[16,128]{1,0:T(8,128)S(1)}, u32[]{:S(2)}, u32[]{:S(2)}) collective-permute-start(s32[16,128]{1,0:T(8,128)S(1)} %concatenate.112), channel_id=1, source_target_pairs={{0,16},{8,24},{16,0},{24,8},{1,17},{9,25},{17,1},{25,9},{2,18},{10... | collective-permute-start | bytes 24584 | tf_op jit(solution)/shard_map/ppermute | solution.py:412

commit v2 on v1

--- a/solution.py
+++ b/solution.py
@@ -83,7 +83,7 @@
         out_shape=[jax.ShapeDtypeStruct(s, BF16) for s in shapes],
         in_specs=[pl.BlockSpec(memory_space=pltpu.VMEM)],
         out_specs=[pl.BlockSpec(memory_space=pltpu.VMEM)] * 4,
-        compiler_params=pltpu.CompilerParams(vmem_limit_bytes=16 * 2**20),
+        compiler_params=pltpu.CompilerParams(vmem_limit_bytes=56 * 2**20),
         name="bands",
     )(wave)
 
@@ -104,15 +104,18 @@
     return out
 
 
-def spread_kernel(cells_ref, out_ref):
+def spread_kernel(cells_ref, instance_ref, out_ref, named_ref):
     own = cells_ref.shape[0]
     for c in range(own // 8):
         tile = cells_ref[pl.ds((c // 8) * 64 + c % 8, 8, stride=8), :]
         for d in range(out_ref.shape[0] // own):
             out_ref[d * own + c * 8 : d * own + c * 8 + 8, :] = tile
-
-
-def pack_kernel(asked_ref, me_ref, cells_ref, early_ref, out_ref):
+    rows = [instance_ref[a : a + 1, :] for a in range(instance_ref.shape[0])]
+    named_ref[...] = jnp.concatenate(rows, axis=1)
+
+
+def pack_kernel(asked_ref, me_ref, cells_ref, *rest):
+    out_ref = rest[-1]
     peers, capacity = asked_ref.shape
 
     @pl.loop(0, peers)
@@ -149,7 +152,8 @@
         out_ref[there, :] = cells_ref[there, :] - STEP_RATE * total
 
 
-def assemble_kernel(index_ref, tiles_ref, target_ref, mask_ref, first_ref, last_ref, turned_ref):
+def assemble_kernel(index_ref, tiles_ref, *rest):
+    mask_ref, first_ref, last_ref, turned_ref = rest[-4:]
     tile_rows, tile_cols = index_ref.shape
     height = tile_rows * TILE
     groups = tile_cols // 4
@@ -169,23 +173,25 @@
         lanes = slice(LANES * g, LANES * (g + 1))
         piece = turned_ref[g * height : (g + 1) * height, :]
         mask_ref[:, lanes] = piece
-        first_ref[: 2 * HALF, lanes] = piece[: 2 * HALF]
-        last_ref[: 2 * HALF, lanes] = piece[height - 2 * HALF :]
-    first_ref[2 * HALF :, :] = target_ref[:HALF, :]
-    last_ref[2 * HALF :, :] = target_ref[height - HALF :, :]
-
-
-def edges_kernel(mask_ref, target_ref, top_ref, bottom_ref, first_ref, last_ref):
+        first_ref[:, lanes] = piece[: 2 * HALF]
+        last_ref[:, lanes] = piece[height - 2 * HALF :]
+
+
+def edges_kernel(mask_ref, top_ref, bottom_ref, first_ref, last_ref):
     height, breadth = mask_ref.shape
     wide = 2 * HALF
-    for ref, lanes in ((first_ref, slice(0, LANES)), (last_ref, slice(breadth - LANES, breadth))):
-        ref[:wide, :] = top_ref[:wide, lanes]
-        ref[wide : wide + height, :] = mask_ref[:, lanes]
-        ref[wide + height : 2 * wide + height, :] = bottom_ref[:wide, lanes]
-        start = 2 * wide + height
-        ref[start : start + HALF, :] = top_ref[wide:, lanes]
-        ref[start + HALF : start + HALF + height, :] = target_ref[:, lanes]
-        ref[start + HALF + height :, :] = bottom_ref[wide:, lanes]
+    half = height // 2
+    lane = lax.broadcasted_iota(jnp.int32, (half + wide, LANES), 1)
+
+    def sides(lanes):
+        upper = jnp.concatenate([top_ref[:, lanes], mask_ref[:half, lanes]], axis=0)
+        lower = jnp.concatenate([mask_ref[half:, lanes], bottom_ref[:, lanes]], axis=0)
+        return upper, lower
+
+    upper, lower = sides(slice(0, LANES))
+    first_ref[...] = jnp.where(lane < wide, upper, pltpu.roll(lower, wide, 1))
+    upper, lower = sides(slice(breadth - LANES, breadth))
+    last_ref[...] = jnp.where(lane < wide, pltpu.roll(upper, wide, 1), lower)
 
 
 def image_kernel(
@@ -193,19 +199,25 @@
     where_ref,
     weight_ref,
     mask_ref,
-    own_ref,
     top_ref,
     bottom_ref,
     before_ref,
     after_ref,
+    target_ref,
+    ttop_ref,
+    tbottom_ref,
+    fcol_hbm,
+    frow_hbm,
+    brow_hbm,
+    bcol_hbm,
+    out_ref,
     fcol_ref,
     frow_ref,
     brow_ref,
     bcol_ref,
-    out_ref,
+    sems,
     mhigh_ref,
     mlow_ref,
-    target_ref,
     field_ref,
     ghigh_ref,
     glow_ref,
@@ -218,55 +230,50 @@
     groups = tile_cols // 4
     wide = 2 * HALF
     block = lax.broadcasted_iota(jnp.int32, (8, LANES), 1) // 32
-
-    def shifted(shift, parts, edge, emit):
-        for rows, ref, start, count in parts:
-            lane = lax.broadcasted_iota(jnp.int32, (count, LANES), 1)
-            turned = None
-            for g in range(groups + 2):
-                if g == 0:
-                    piece = before_ref[edge + rows : edge + rows + count, :]
-                elif g == groups + 1:
-                    piece = after_ref[edge + rows : edge + rows + count, :]
-                else:
-                    piece = ref[start : start + count, LANES * (g - 1) : LANES * g]
-                fresh = pltpu.roll(piece, shift, 1)
-                if g:
-                    emit(rows, count, g - 1, jnp.where(lane < shift, turned, fresh))
-                turned = fresh
-
-    def put_mask(rows, count, g, piece):
-        high, low = split(piece)
-        mhigh_ref[rows : rows + count, LANES * g : LANES * (g + 1)] = high
-        mlow_ref[rows : rows + count, LANES * g : LANES * (g + 1)] = low
-
-    def put_target(rows, count, g, piece):
-        target_ref[rows : rows + count, LANES * g : LANES * (g + 1)] = piece
-
-    shifted(
-        wide,
-        (
-            (0, top_ref, 0, wide),
-            (wide, mask_ref, 0, rows_here),
-            (wide + rows_here, bottom_ref, 0, wide),
-        ),
-        0,
-        put_mask,
-    )
-    shifted(
-        HALF,
-        (
-            (0, top_ref, wide, HALF),
-            (HALF, own_ref, 0, rows_here),
-            (HALF + rows_here, bottom_ref, wide, HALF),
-        ),
-        high_rows,
-        put_target,
-    )
+    fetches = [
+        pltpu.make_async_copy(source, there, sems.at[n])
+        for n, (source, there) in enumerate(
+            (
+                (fcol_hbm, fcol_ref),
+                (frow_hbm, frow_ref),
+                (brow_hbm, brow_ref),
+                (bcol_hbm, bcol_ref),
+            )
+        )
+    ]
+    for fetch in fetches:
+        fetch.start()
+
+    lane = lax.broadcasted_iota(jnp.int32, (wide, LANES), 1)
+    for rows in range(0, high_rows, wide):
+        if rows == 0:
+            ref, start = top_ref, 0
+        elif rows == high_rows - wide:
+            ref, start = bottom_ref, 0
+        else:
+            ref, start = mask_ref, rows - wide
+        half = high_rows // 2
+        edge = slice(rows % half, rows % half + wide)
+        turned = before_ref[edge, :]
+        final = after_ref[edge, :]
+        if rows < half:
+            final = pltpu.roll(final, wide, 1)
+        else:
+            turned = pltpu.roll(turned, wide, 1)
+        for g in range(groups + 1):
+            fresh = final
+            if g < groups:
+                fresh = pltpu.roll(ref[start : start + wide, LANES * g : LANES * (g + 1)], wide, 1)
+            high, low = split(jnp.where(lane < wide, turned, fresh))
+            mhigh_ref[rows : rows + wide, LANES * g : LANES * (g + 1)] = high
+            mlow_ref[rows : rows + wide, LANES * g : LANES * (g + 1)] = low
+            turned = fresh
     for g in range(groups + 1, mhigh_ref.shape[1] // LANES):
         lanes = slice(LANES * g, LANES * (g + 1))
         mhigh_ref[:, lanes] = jnp.zeros((high_rows, LANES), BF16)
         mlow_ref[:, lanes] = jnp.zeros((high_rows, LANES), BF16)
+    for fetch in fetches[:3]:
+        fetch.wait()
 
     def columns(offset, width):
         def window(ref, j):
@@ -305,7 +312,10 @@
                 term = weight_ref[k] * field * field
                 intensity = term if intensity is None else intensity + term
         resist = 1.0 / (1.0 + jnp.exp(-STEEPNESS * (intensity - THRESHOLD)))
-        target = target_ref[:, pl.ds(pl.multiple_of(offset, LANES), width)]
+        place = pl.ds(pl.multiple_of(offset, LANES), width)
+        target = jnp.concatenate(
+            [ttop_ref[:, place], target_ref[:, place], tbottom_ref[:, place]], axis=0
+        )
         sensitivity = 2.0 * (resist - target) * STEEPNESS * resist * (1.0 - resist)
         row = where_ref[0] + lax.broadcasted_iota(jnp.int32, (field_rows, width), 0)
         col = where_ref[1] + offset + lax.broadcasted_iota(jnp.int32, (field_rows, width), 1)
@@ -318,7 +328,6 @@
             both = mm(jnp.concatenate([near, brow_ref[k, 1, :, :field_rows]], axis=0), high)
             part = both[:rows_here] + both[rows_here:] + mm(near, low)
             high, low = split(part)
-            place = pl.ds(pl.multiple_of(offset, LANES), width)
             ghigh_ref[k, :, place] = high
             glow_ref[k, :, place] = low
 
@@ -329,6 +338,7 @@
         columns(jj * WIDE, WIDE)
 
     columns(supers * WIDE, LANES)
+    fetches[3].wait()
 
     def spread_back(k):
         def window(ref, jj):
@@ -380,7 +390,7 @@
     return x.reshape(count // 8, 8, 8, LANES).transpose(0, 2, 1, 3).reshape(count, 8 * LANES)
 
 
-def kernel_call(body, name, shapes, scratch, scalars, inputs, megabytes, unread=()):
+def kernel_call(body, name, shapes, scratch, scalars, inputs, unread=()):
     single = not isinstance(shapes, list)
     spec = pl.BlockSpec(memory_space=pltpu.VMEM)
     outs = [shapes] if single else shapes
@@ -392,7 +402,7 @@
         + [pl.BlockSpec(memory_space=pl.ANY)] * len(unread),
         out_specs=[spec] * len(outs),
         scratch_shapes=scratch,
-        compiler_params=pltpu.CompilerParams(vmem_limit_bytes=megabytes * 2**20),
+        compiler_params=pltpu.CompilerParams(vmem_limit_bytes=56 * 2**20),
         name=name,
     )(*scalars, *inputs, *unread)
     return result[0] if single else result
@@ -436,18 +446,29 @@
     f32 = lambda *shape: jax.ShapeDtypeStruct(shape, F32)
 
     flat = to_rows(cells)
-    copies = kernel_call(
-        spread_kernel, "spread", f32(deep * slots * 8, LANES), [], [], [flat], 8
+    copies, named = kernel_call(
+        spread_kernel,
+        "spread",
+        [
+            f32(deep * slots * 8, LANES),
+            jax.ShapeDtypeStruct((1, tiles_here), jnp.int32),
+        ],
+        [],
+        [],
+        [flat, instance_cell],
     )
     stack = lax.all_to_all(copies, "deep", split_axis=0, concat_axis=0, tiled=True)
 
-    named = instance_cell.reshape(1, -1)
     near = doubled(doubled(named, "col"), "core")
     me = jnp.stack([lax.axis_index(plane), lax.axis_index(everyone)]).astype(jnp.int32)
     owner = near // slots
     asked = requests(
         owner % peers == me[0], (owner // peers) * slots + near % slots, wide_capacity
     )
+    sides = lax.optimization_barrier((target, named))[0]
+    left, right = neighbours(sides[:, :HALF], sides[:, breadth - HALF :], "col")
+    blank = jnp.zeros((height, LANES - 2 * HALF), F32)
+    wide_target = jnp.concatenate([left, target, right, blank], axis=1)
     bands = make_bands(row_taps, col_taps)
     packed = kernel_call(
         pack_kernel,
@@ -456,13 +477,14 @@
         [],
         [asked, me],
         [stack],
-        8,
-        [bands[0]],
-    )
+        [bands[0], wide_target],
+    )
+    packed, near, wide_target = lax.optimization_barrier((packed, near, wide_target))
     arrived = lax.all_to_all(packed, plane, split_axis=0, concat_axis=0, tiled=True)
 
     everything = doubled(near, "deep")
     wanted = requests(everything // slots == me[1], everything % slots, capacity)
+    above, below = neighbours(wide_target[:HALF], wide_target[height - HALF :], ("deep", "core"))
     mine = named[0] // slots
     earlier = jnp.tri(tiles_here, k=-1, dtype=bool)
 
@@ -474,23 +496,15 @@
     mask, first, last = kernel_call(
         assemble_kernel,
         "assemble",
-        [f32(height, breadth), f32(3 * HALF, breadth), f32(3 * HALF, breadth)],
+        [f32(height, breadth), f32(2 * HALF, breadth), f32(2 * HALF, breadth)],
         [pltpu.VMEM((height * (breadth // LANES), LANES), F32)],
         [place(mine % peers, wide_capacity)],
-        [arrived, target],
-        8,
+        [arrived],
+        [wanted, above, below],
     )
     top, bottom = neighbours(first, last, ("deep", "core"))
-    edge_rows = 2 * height + 6 * HALF
-    first, last = kernel_call(
-        edges_kernel,
-        "edges",
-        [f32(edge_rows, LANES), f32(edge_rows, LANES)],
-        [],
-        [],
-        [mask, target, top, bottom],
-        8,
-    )
+    edge = f32(height // 2 + 2 * HALF, LANES)
+    first, last = kernel_call(edges_kernel, "edges", [edge, edge], [], [], [mask, top, bottom])
     before, after = neighbours(first, last, "col")
     my_row = lax.axis_index(("deep", "core"))
     my_col = lax.axis_index("col")
@@ -507,18 +521,19 @@
         image_kernel,
         "image",
         f32(owners * capacity * 8, LANES),
-        [
+        [pltpu.VMEM(band.shape, BF16) for band in bands]
+        + [
+            pltpu.SemaphoreType.DMA((4,)),
             pltpu.VMEM((height + 4 * HALF, breadth + 256), BF16),
             pltpu.VMEM((height + 4 * HALF, breadth + 256), BF16),
-            pltpu.VMEM((field_rows, breadth + 128), F32),
             pltpu.VMEM((KERNELS, field_rows, WIDE), F32),
             pltpu.VMEM((KERNELS, height, breadth + 128), BF16),
             pltpu.VMEM((KERNELS, height, breadth + 128), BF16),
             pltpu.VMEM((height * (breadth // LANES), LANES), F32),
         ],
         [place(mine, capacity), where, kernel_weight],
-        [mask, target, top, bottom, before, after, *bands],
-        32,
+        [mask, top, bottom, before, after, wide_target, above, below],
+        bands,
     )
     back = lax.all_to_all(returned, everyone, split_axis=0, concat_axis=0, tiled=True)
     stepped = kernel_call(
@@ -528,7 +543,6 @@
         [pltpu.VMEM((slots * 8, LANES), F32)] * 4,
         [wanted, me],
         [flat, back],
-        8,
     )
     return from_rows(stepped)
 

time: 136 us -> 149 us (1.096)
  blocking collectives: 0 us -> 35.4 us
  waiting for transfers between devices: 49.2 us -> 13.9 us
  Pallas kernels: 33.5 us -> 45.1 us
  other arithmetic: 3.31 us -> 11.3 us
  local copies, waits for them, and re-layouts: 13 us -> 7.14 us
  starting transfers between devices: 36.6 us -> 35 us
    all_to_all x0 -> x1, blocking collectives: none -> 35.4 us  [shards(): lax.all_to_all(returned, everyone, split_axis=0, concat_axis=0, tiled=True)]
    ppermute x5, waiting for transfers between devices: 21.4 us -> 2.93 us  [doubled(): got = lax.ppermute(table, axis, [(i, i ^ bit) for i in range(count)])]
    ppermute x4 -> x8, starting transfers between devices: 7.51 us -> 17.6 us  [neighbours(): return (lax.ppermute(last, axis, up), lax.ppermute(first, axis, down))]
    all_to_all x1, waiting for transfers between devices: 14.3 us -> 4.21 us  [shards(): lax.all_to_all(packed, plane, split_axis=0, concat_axis=0, tiled=True)]
    all_to_all x1 -> x0, starting transfers between devices: 9.24 us -> none  [shards(): lax.all_to_all(returned, everyone, split_axis=0, concat_axis=0, tiled=True)]
    unnamed x28 -> x20, local copies, waits for them, and re-layouts: 11.8 us -> 3.17 us
    pallas_call x6, Pallas kernels: 31.9 us -> 40 us  [kernel_call(): pl.pallas_call(body, out_shape=outs, in_specs=[pl.BlockSpec(memory_space=...]
    ppermute x5, starting transfers between devices: 11.1 us -> 7.46 us  [doubled(): got = lax.ppermute(table, axis, [(i, i ^ bit) for i in range(count)])]
  transfers between devices with their start and end apart: 12 -> 15, of which waited for: 8 -> 6; matrix products, arithmetic and copies ran while one was open for 3% -> 10% of each run, Pallas kernels for 2% -> 3%
where the time goes in v2:
time: 149 us; the launch traced here: 148 us
  Pallas kernels  45.1 us (30%)
  blocking collectives  35.4 us (24%)
  starting transfers between devices  35 us (23%)
  waiting for transfers between devices  13.9 us (9%)
  other arithmetic  11.3 us (8%)
  local copies, waits for them, and re-layouts  7.14 us (5%)
    pallas_call x6, Pallas kernels, kernel_call(): pl.pallas_call(body, out_shape=outs, in_specs=[pl.BlockSpec(memory_space=...  40 us
    all_to_all x1, blocking collectives, shards(): lax.all_to_all(returned, everyone, split_axis=0, concat_axis=0, tiled=True)  35.4 us
    ppermute x8, starting transfers between devices, neighbours(): return (lax.ppermute(last, axis, up), lax.ppermute(first, axis, down))  17.6 us
    ppermute x5, starting transfers between devices, doubled(): got = lax.ppermute(table, axis, [(i, i ^ bit) for i in range(count)])  7.46 us
    ppermute x8, waiting for transfers between devices, neighbours(): return (lax.ppermute(last, axis, up), lax.ppermute(first, axis, down))  6.74 us
    all_to_all x1, starting transfers between devices, shards(): lax.all_to_all(copies, 'deep', split_axis=0, concat_axis=0, tiled=True)  6.32 us
    pallas_call x1, Pallas kernels, make_bands(): pl.pallas_call(bands_kernel, out_shape=[jax.ShapeDtypeStruct(s, BF16) for...  5.1 us
    all_to_all x1, waiting for transfers between devices, shards(): lax.all_to_all(packed, plane, split_axis=0, concat_axis=0, tiled=True)  4.21 us
  transfers between devices with their start and end apart: 15, of which 6 were waited for; matrix products, arithmetic and copies ran while one was open for 10% of the time, Pallas kernels for 3%

profile of v2, /device:TPU:0, one launch (start us, length us, event | category | flops | bytes accessed | tf_op | source)
XLA Modules:
  0.0 148.0 jit_solution(6631371774418270407)
XLA Ops:
  0.0 1.7 %spread.1 = (f32[1024,128]{1,0:T(8,128)}, s32[1,128]{1,0:T(1,128)}) custom-call(f32[256,128]{1,0:T(8,128)} %bitcast.37, s32[4,32]{1,0:T(4,128)} %instance_ref.1), custom_call_target="tpu_custom_call" | custom-call | tf_op jit(solution)/shard_map/spread/pallas_call | solution.py:397
  1.7 6.3 %all-to-all-start = ((f32[4,256,128]{2,1,0:T(8,128)}), f32[4,256,128]{2,1,0:T(8,128)S(1)}, u32[]{:S(2)}, u32[]{:S(2)}) async-start(f32[4,256,128]{2,1,0:T(8,128)} %bitcast.39), calls=%async_computation | async-start | bytes 1048576 | tf_op jit(solution)/shard_map/all_to_all | solution.py:460
  8.1 1.5 %collective-permute-start = (s32[1,128]{1,0:T(1,128)}, s32[1,128]{1,0:T(1,128)S(1)}, u32[]{:S(2)}, u32[]{:S(2)}) collective-permute-start(s32[1,128]{1,0:T(1,128)} %get-tuple-element.20), channel_id=1, source_target_pairs={{0,1},{1,0},{2,3},{3,2},{4,5},{5,4},{6,7},{7,6},{8,9},{9,8},{10,11... | collective-permute-start | bytes 1544 | tf_op jit(solution)/shard_map/ppermute | solution.py:422
  9.5 1.0 fusion.27
  10.5 1.3 collective-permute-start.4
  11.8 4.5 %collective-permute-start.3 = (f32[128,32]{1,0:T(8,128)S(1)}, f32[128,32]{1,0:T(8,128)S(1)}, u32[]{:S(2)}, u32[]{:S(2)}) collective-permute-start(f32[128,32]{1,0:T(8,128)S(1)} %get-tuple-element.48), channel_id=1, source_target_pairs={{0,1},{1,2},{2,3},{4,5},{5,6},{6,7},{8,9},{9,10},{10,11},{12,13},{... | collective-permute-start | bytes 49160 | tf_op jit(solution)/shard_map/ppermute | solution.py:415
  17.5 1.3 fusion.19
  21.3 1.5 %collective-permute-start.1 = (s32[2,128]{1,0:T(2,128)S(1)}, s32[2,128]{1,0:T(2,128)S(1)}, u32[]{:S(2)}, u32[]{:S(2)}) collective-permute-start(s32[2,128]{1,0:T(2,128)S(1)} %pad_add_fusion.3), channel_id=1, source_target_pairs={{0,2},{1,3},{2,0},{3,1},{4,6},{5,7},{6,4},{7,5},{8,10},{9,11},{10,... | collective-permute-start | bytes 3080 | tf_op jit(solution)/shard_map/ppermute | solution.py:422
  22.8 1.3 select_maximum_fusion.wave_ref
  26.2 5.1 %bands.1 = (bf16[8,2,256,128]{3,2,1,0:T(8,128)(2,1)}, bf16[8,2,192,256]{3,2,1,0:T(8,128)(2,1)}, bf16[8,2,128,256]{3,2,1,0:T(8,128)(2,1)}, bf16[8,2,384,256]{3,2,1,0:T(8,128)(2,1)}) custom-call(f32[32,128]{1,0:T(8,128)} %select_maximum_fusion.wave_ref), custom_call_target="tpu_custom_call" | custom-call | tf_op jit(solution)/shard_map/bands/pallas_call | solution.py:81
  33.7 2.2 %concatenate.113.rest_1_.target_ref = f32[128,1152]{1,0:T(8,128)} concatenate(f32[128,32]{1,0:T(8,128)S(1)} %collective-permute-done.3, f32[128,1024]{1,0:T(8,128)} %param.8, f32[128,32]{1,0:T(8,128)S(1)} %collective-permute-done.4, f32[128,64]{1,0:T(8,128)S(1)} %broadcast_in_dim.28), dimensions={1} | concatenate | bytes 1179648 | tf_op jit(solution)/shard_map/concatenate | solution.py:471
  36.7 2.5 %pack.1 = f32[2048,128]{1,0:T(8,128)} custom-call(s32[8,32]{1,0:T(8,128)} %select_reduce_fusion.1.asked_ref, s32[2]{0:T(128)} %pad_add_fusion.4.me_ref, f32[1024,128]{1,0:T(8,128)} %bitcast.36, bf16[8,2,256,128]{3,2,1,0:T(8,128)(2,1)} %get-tuple-element.22.rest_0_.fcol_hbm, f32[128,1152]{1,0:T(8,128)} %concatenate.113.rest_1_.target_ref), custom_call_target="tpu_custom_call" | custom-call | tf_op jit(solution)/shard_map/pack/pallas_call | solution.py:397
  39.2 2.0 %collective-permute-start.5 = (s32[8,128]{1,0:T(8,128)S(1)}, s32[8,128]{1,0:T(8,128)S(1)}, u32[]{:S(2)}, u32[]{:S(2)}) collective-permute-start(s32[8,128]{1,0:T(8,128)S(1)} %get-tuple-element.24), channel_id=1, source_target_pairs={{0,8},{8,0},{16,24},{24,16},{1,9},{9,1},{17,25},{25,17},{2,10},{10... | collective-permute-start | bytes 12296 | tf_op jit(solution)/shard_map/ppermute | solution.py:422
  41.3 3.6 %all-to-all-start.1 = ((f32[8,256,128]{2,1,0:T(8,128)}), f32[8,256,128]{2,1,0:T(8,128)S(1)}, u32[]{:S(2)}, u32[]{:S(2)}) async-start(f32[8,256,128]{2,1,0:T(8,128)} %bitcast.34), calls=%async_computation.1 | async-start | bytes 2097152 | tf_op jit(solution)/shard_map/all_to_all | solution.py:483
  44.9 1.3 collective-permute-start.8
  46.2 3.0 %collective-permute-start.7 = (f32[32,1152]{1,0:T(8,128)S(1)}, f32[32,1152]{1,0:T(8,128)S(1)}, u32[]{:S(2)}, u32[]{:S(2)}) collective-permute-start(f32[32,1152]{1,0:T(8,128)S(1)} %get-tuple-element.46), channel_id=1, source_target_pairs={{0,4},{4,8},{8,12},{12,16},{16,20},{20,24},{24,28},{1,5},{5,9},{9,... | collective-permute-start | bytes 442376 | tf_op jit(solution)/shard_map/ppermute | solution.py:415
  49.2 2.4 %collective-permute-start.6 = (s32[16,128]{1,0:T(8,128)S(1)}, s32[16,128]{1,0:T(8,128)S(1)}, u32[]{:S(2)}, u32[]{:S(2)}) collective-permute-start(s32[16,128]{1,0:T(8,128)S(1)} %pad_add_fusion), channel_id=1, source_target_pairs={{0,16},{8,24},{16,0},{24,8},{1,17},{9,25},{17,1},{25,9},{2,18},{10... | collective-permute-start | bytes 24584 | tf_op jit(solution)/shard_map/ppermute | solution.py:422
  51.6 2.2 %collective-permute-done.6 = s32[16,128]{1,0:T(8,128)S(1)} collective-permute-done((s32[16,128]{1,0:T(8,128)S(1)}, s32[16,128]{1,0:T(8,128)S(1)}, u32[]{:S(2)}, u32[]{:S(2)}) %collective-permute-start.6) | collective-permute-done | bytes 8224 | tf_op jit(solution)/shard_map/ppermute | solution.py:422
  54.2 1.2 select_reduce_fusion.rest_0_.asked_ref
  55.4 4.2 %all-to-all-done.1 = f32[8,256,128]{2,1,0:T(8,128)S(1)} async-done(((f32[8,256,128]{2,1,0:T(8,128)}), f32[8,256,128]{2,1,0:T(8,128)S(1)}, u32[]{:S(2)}, u32[]{:S(2)}) %all-to-all-start.1) | async-done | bytes 1048608 | tf_op jit(solution)/shard_map/all_to_all | solution.py:483
  59.6 1.0 copy-done.1
  60.6 2.8 %assemble.1 = (f32[128,1024]{1,0:T(8,128)}, f32[64,1024]{1,0:T(8,128)}, f32[64,1024]{1,0:T(8,128)}) custom-call(s32[4,32]{1,0:T(4,128)} %get-tuple-element.51.index_ref, f32[2048,128]{1,0:T(8,128)} %bitcast.32, s32[32,8]{1,0:T(8,128)} %select_reduce_fusion.rest_0_.asked_ref, f32[32,1152]{1,0:T(8,128)} %copy-done.6, f32[32,1152]{1,0:T(8,128)} %copy-done.5), custom_call_target="tpu_custom_call" | custom-call | tf_op jit(solution)/shard_map/assemble/pallas_call | solution.py:397
  63.4 2.2 %collective-permute-start.9 = (f32[64,1024]{1,0:T(8,128)}, f32[64,1024]{1,0:T(8,128)S(1)}, u32[]{:S(2)}, u32[]{:S(2)}) collective-permute-start(f32[64,1024]{1,0:T(8,128)} %get-tuple-element.28), channel_id=1, source_target_pairs={{0,4},{4,8},{8,12},{12,16},{16,20},{20,24},{24,28},{1,5},{5,9},{9,... | collective-permute-start | bytes 786440 | tf_op jit(solution)/shard_map/ppermute | solution.py:415
  65.6 1.3 collective-permute-start.10
  66.9 2.3 %collective-permute-done.10.bottom_ref = f32[64,1024]{1,0:T(8,128)S(1)} collective-permute-done((f32[64,1024]{1,0:T(8,128)}, f32[64,1024]{1,0:T(8,128)S(1)}, u32[]{:S(2)}, u32[]{:S(2)}) %collective-permute-start.10) | collective-permute-done | bytes 262176 | tf_op jit(solution)/shard_map/ppermute | solution.py:415
  69.9 1.9 %edges.1 = (f32[128,128]{1,0:T(8,128)}, f32[128,128]{1,0:T(8,128)}) custom-call(f32[128,1024]{1,0:T(8,128)} %get-tuple-element.27.mask_ref, f32[64,1024]{1,0:T(8,128)} %copy-done.3, f32[64,1024]{1,0:T(8,128)} %copy-done.4), custom_call_target="tpu_custom_call" | custom-call | tf_op jit(solution)/shard_map/edges/pallas_call | solution.py:397
  71.8 2.7 %collective-permute-start.11 = (f32[128,128]{1,0:T(8,128)}, f32[128,128]{1,0:T(8,128)S(1)}, u32[]{:S(2)}, u32[]{:S(2)}) collective-permute-start(f32[128,128]{1,0:T(8,128)} %get-tuple-element.30), channel_id=1, source_target_pairs={{0,1},{1,2},{2,3},{4,5},{5,6},{6,7},{8,9},{9,10},{10,11},{12,13},{... | collective-permute-start | bytes 196616 | tf_op jit(solution)/shard_map/ppermute | solution.py:415
  74.5 1.3 collective-permute-start.12
  76.7 4.2 %collective-permute-done.12.after_ref = f32[128,128]{1,0:T(8,128)S(1)} collective-permute-done((f32[128,128]{1,0:T(8,128)}, f32[128,128]{1,0:T(8,128)S(1)}, u32[]{:S(2)}, u32[]{:S(2)}) %collective-permute-start.12) | collective-permute-done | bytes 65568 | tf_op jit(solution)/shard_map/ppermute | solution.py:415
  81.5 28.2 %image.1 = f32[2048,128]{1,0:T(8,128)} custom-call(s32[4,32]{1,0:T(4,128)} %get-tuple-element.52.index_ref, s32[4]{0:T(128)} %pad_add_fusion.5.where_ref, f32[8]{0:T(128)} %weight_ref.1, f32[128,1024]{1,0:T(8,128)} %get-tuple-element.27.mask_ref, f32[64,1024]{1,0:T(8,128)} %copy-done.3, f32[64,1024]{1,0:T(8,128)} %copy-done.4, f32[128,128]{1,0:T(8,128)} %copy-done.7, ...), custom_call_target="tpu_custom_call" | custom-call | tf_op jit(solution)/shard_map/image/pallas_call | solution.py:397
  109.7 35.4 %all_to_all.33 = f32[32,64,128]{2,1,0:T(8,128)} all-to-all(f32[32,64,128]{2,1,0:T(8,128)} %bitcast.35), channel_id=1, replica_groups=mesh['deep'=4,'core'=2,'col'=4] {'deep','core','col'}, dimensions={0} | all-to-all | bytes 2097152 | tf_op jit(solution)/shard_map/all_to_all | solution.py:538
  145.1 2.9 %step.1 = f32[256,128]{1,0:T(8,128)} custom-call(s32[32,8]{1,0:T(8,128)} %select_reduce_fusion.rest_0_.asked_ref, s32[2]{0:T(128)} %pad_add_fusion.4.me_ref, f32[256,128]{1,0:T(8,128)} %bitcast.38, f32[2048,128]{1,0:T(8,128)} %bitcast.33), custom_call_target="tpu_custom_call" | custom-call | tf_op jit(solution)/shard_map/step/pallas_call | solution.py:397
  (57 shorter events, 11.6 us)
Async XLA Ops:
  1.7 34.1 %all-to-all-start = ((f32[4,256,128]{2,1,0:T(8,128)}), f32[4,256,128]{2,1,0:T(8,128)S(1)}, u32[]{:S(2)}, u32[]{:S(2)}) async-start(f32[4,256,128]{2,1,0:T(8,128)} %bitcast.39), calls=%async_computation | async-start | bytes 1048576 | tf_op jit(solution)/shard_map/all_to_all | solution.py:460
  8.1 12.6 %collective-permute-start = (s32[1,128]{1,0:T(1,128)}, s32[1,128]{1,0:T(1,128)S(1)}, u32[]{:S(2)}, u32[]{:S(2)}) collective-permute-start(s32[1,128]{1,0:T(1,128)} %get-tuple-element.20), channel_id=1, source_target_pairs={{0,1},{1,0},{2,3},{3,2},{4,5},{5,4},{6,7},{7,6},{8,9},{9,8},{10,11... | collective-permute-start | bytes 1544 | tf_op jit(solution)/shard_map/ppermute | solution.py:422
  10.5 23.2 %collective-permute-start.4 = (f32[128,32]{1,0:T(8,128)S(1)}, f32[128,32]{1,0:T(8,128)S(1)}, u32[]{:S(2)}, u32[]{:S(2)}) collective-permute-start(f32[128,32]{1,0:T(8,128)S(1)} %get-tuple-element.47), channel_id=1, source_target_pairs={{1,0},{2,1},{3,2},{5,4},{6,5},{7,6},{9,8},{10,9},{11,10},{13,12},{... | collective-permute-start | bytes 49160 | tf_op jit(solution)/shard_map/ppermute | solution.py:415
  11.8 21.9 %collective-permute-start.3 = (f32[128,32]{1,0:T(8,128)S(1)}, f32[128,32]{1,0:T(8,128)S(1)}, u32[]{:S(2)}, u32[]{:S(2)}) collective-permute-start(f32[128,32]{1,0:T(8,128)S(1)} %get-tuple-element.48), channel_id=1, source_target_pairs={{0,1},{1,2},{2,3},{4,5},{5,6},{6,7},{8,9},{9,10},{10,11},{12,13},{... | collective-permute-start | bytes 49160 | tf_op jit(solution)/shard_map/ppermute | solution.py:415
  21.3 3.6 %collective-permute-start.1 = (s32[2,128]{1,0:T(2,128)S(1)}, s32[2,128]{1,0:T(2,128)S(1)}, u32[]{:S(2)}, u32[]{:S(2)}) collective-permute-start(s32[2,128]{1,0:T(2,128)S(1)} %pad_add_fusion.3), channel_id=1, source_target_pairs={{0,2},{1,3},{2,0},{3,1},{4,6},{5,7},{6,4},{7,5},{8,10},{9,11},{10,... | collective-permute-start | bytes 3080 | tf_op jit(solution)/shard_map/ppermute | solution.py:422
  25.5 5.8 %collective-permute-start.2 = (s32[4,128]{1,0:T(4,128)S(1)}, s32[4,128]{1,0:T(4,128)S(1)}, u32[]{:S(2)}, u32[]{:S(2)}) collective-permute-start(s32[4,128]{1,0:T(4,128)S(1)} %pad_add_fusion.2), channel_id=1, source_target_pairs={{0,4},{4,0},{1,5},{5,1},{2,6},{6,2},{3,7},{7,3},{8,12},{12,8},{9,1... | collective-permute-start | bytes 6152 | tf_op jit(solution)/shard_map/ppermute | solution.py:422
  35.9 8.9 %copy-start = (f32[128,1152]{1,0:T(8,128)S(1)}, f32[128,1152]{1,0:T(8,128)}, u32[]{:S(2)}) copy-start(f32[128,1152]{1,0:T(8,128)} %concatenate.113.rest_1_.target_ref) | copy-start | bytes 1769476
  35.9 0.9 copy-start.2
  39.2 10.0 %collective-permute-start.5 = (s32[8,128]{1,0:T(8,128)S(1)}, s32[8,128]{1,0:T(8,128)S(1)}, u32[]{:S(2)}, u32[]{:S(2)}) collective-permute-start(s32[8,128]{1,0:T(8,128)S(1)} %get-tuple-element.24), channel_id=1, source_target_pairs={{0,8},{8,0},{16,24},{24,16},{1,9},{9,1},{17,25},{25,17},{2,10},{10... | collective-permute-start | bytes 12296 | tf_op jit(solution)/shard_map/ppermute | solution.py:422
  41.3 18.4 %all-to-all-start.1 = ((f32[8,256,128]{2,1,0:T(8,128)}), f32[8,256,128]{2,1,0:T(8,128)S(1)}, u32[]{:S(2)}, u32[]{:S(2)}) async-start(f32[8,256,128]{2,1,0:T(8,128)} %bitcast.34), calls=%async_computation.1 | async-start | bytes 2097152 | tf_op jit(solution)/shard_map/all_to_all | solution.py:483
  44.9 10.5 %collective-permute-start.8 = (f32[32,1152]{1,0:T(8,128)S(1)}, f32[32,1152]{1,0:T(8,128)S(1)}, u32[]{:S(2)}, u32[]{:S(2)}) collective-permute-start(f32[32,1152]{1,0:T(8,128)S(1)} %get-tuple-element.45), channel_id=1, source_target_pairs={{4,0},{8,4},{12,8},{16,12},{20,16},{24,20},{28,24},{5,1},{9,5},{13... | collective-permute-start | bytes 442376 | tf_op jit(solution)/shard_map/ppermute | solution.py:415
  46.2 9.2 %collective-permute-start.7 = (f32[32,1152]{1,0:T(8,128)S(1)}, f32[32,1152]{1,0:T(8,128)S(1)}, u32[]{:S(2)}, u32[]{:S(2)}) collective-permute-start(f32[32,1152]{1,0:T(8,128)S(1)} %get-tuple-element.46), channel_id=1, source_target_pairs={{0,4},{4,8},{8,12},{12,16},{16,20},{20,24},{24,28},{1,5},{5,9},{9,... | collective-permute-start | bytes 442376 | tf_op jit(solution)/shard_map/ppermute | solution.py:415
  49.2 4.6 %collective-permute-start.6 = (s32[16,128]{1,0:T(8,128)S(1)}, s32[16,128]{1,0:T(8,128)S(1)}, u32[]{:S(2)}, u32[]{:S(2)}) collective-permute-start(s32[16,128]{1,0:T(8,128)S(1)} %pad_add_fusion), channel_id=1, source_target_pairs={{0,16},{8,24},{16,0},{24,8},{1,17},{9,25},{17,1},{25,9},{2,18},{10... | collective-permute-start | bytes 24584 | tf_op jit(solution)/shard_map/ppermute | solution.py:422
  55.4 4.2 %copy-start.5 = (f32[32,1152]{1,0:T(8,128)}, f32[32,1152]{1,0:T(8,128)S(1)}, u32[]{:S(2)}) copy-start(f32[32,1152]{1,0:T(8,128)S(1)} %collective-permute-done.8.rest_2_.tbottom_ref) | copy-start | bytes 442372
  55.4 4.2 %copy-start.6 = (f32[32,1152]{1,0:T(8,128)}, f32[32,1152]{1,0:T(8,128)S(1)}, u32[]{:S(2)}) copy-start(f32[32,1152]{1,0:T(8,128)S(1)} %collective-permute-done.7.rest_1_.ttop_ref) | copy-start | bytes 442372
  59.6 1.0 copy-start.1
  63.4 3.5 %collective-permute-start.9 = (f32[64,1024]{1,0:T(8,128)}, f32[64,1024]{1,0:T(8,128)S(1)}, u32[]{:S(2)}, u32[]{:S(2)}) collective-permute-start(f32[64,1024]{1,0:T(8,128)} %get-tuple-element.28), channel_id=1, source_target_pairs={{0,4},{4,8},{8,12},{12,16},{16,20},{20,24},{24,28},{1,5},{5,9},{9,... | collective-permute-start | bytes 786440 | tf_op jit(solution)/shard_map/ppermute | solution.py:415
  65.6 3.6 %collective-permute-start.10 = (f32[64,1024]{1,0:T(8,128)}, f32[64,1024]{1,0:T(8,128)S(1)}, u32[]{:S(2)}, u32[]{:S(2)}) collective-permute-start(f32[64,1024]{1,0:T(8,128)} %get-tuple-element.29), channel_id=1, source_target_pairs={{4,0},{8,4},{12,8},{16,12},{20,16},{24,20},{28,24},{5,1},{9,5},{13... | collective-permute-start | bytes 786440 | tf_op jit(solution)/shard_map/ppermute | solution.py:415
  66.9 2.3 %copy-start.3 = (f32[64,1024]{1,0:T(8,128)}, f32[64,1024]{1,0:T(8,128)S(1)}, u32[]{:S(2)}) copy-start(f32[64,1024]{1,0:T(8,128)S(1)} %collective-permute-done.9.top_ref) | copy-start | bytes 786436
  69.2 0.7 copy-start.4
  71.8 4.9 %collective-permute-start.11 = (f32[128,128]{1,0:T(8,128)}, f32[128,128]{1,0:T(8,128)S(1)}, u32[]{:S(2)}, u32[]{:S(2)}) collective-permute-start(f32[128,128]{1,0:T(8,128)} %get-tuple-element.30), channel_id=1, source_target_pairs={{0,1},{1,2},{2,3},{4,5},{5,6},{6,7},{8,9},{9,10},{10,11},{12,13},{... | collective-permute-start | bytes 196616 | tf_op jit(solution)/shard_map/ppermute | solution.py:415
  74.5 6.4 %collective-permute-start.12 = (f32[128,128]{1,0:T(8,128)}, f32[128,128]{1,0:T(8,128)S(1)}, u32[]{:S(2)}, u32[]{:S(2)}) collective-permute-start(f32[128,128]{1,0:T(8,128)} %get-tuple-element.31), channel_id=1, source_target_pairs={{1,0},{2,1},{3,2},{5,4},{6,5},{7,6},{9,8},{10,9},{11,10},{13,12},{... | collective-permute-start | bytes 196616 | tf_op jit(solution)/shard_map/ppermute | solution.py:415
  76.7 4.2 %copy-start.7 = (f32[128,128]{1,0:T(8,128)}, f32[128,128]{1,0:T(8,128)S(1)}, u32[]{:S(2)}) copy-start(f32[128,128]{1,0:T(8,128)S(1)} %collective-permute-done.11.before_ref) | copy-start | bytes 196612
  80.9 0.6 copy-start.8
